TPU v7x, 32 devices: a whole 2x2x4 slice. The times are simulated.
32 devices in a mesh: strike: 8 (over z, y), dip: 4 (over x, core).
Axes of the slice: x: 2, y: 2, z: 4, core: 2. Of those that a mesh axis runs over, the one named last changes fastest.
Arguments:
- slip_rate: float32 [3, 4096, 1024], P(None, 'strike', 'dip'), may hold values from -6 to 6
- history: bfloat16 [4, 3, 2, 1024, 4096], P(None, None, None, ('strike', 'dip')), may hold values from -6 to 6
- lengths: int32 [1024, 4096], P(('strike', 'dip')), may hold values from 1 to 4, as said below
- prestress: float32 [2, 4096, 1024], P(None, 'strike', 'dip'), may hold values from -8 to 8
- normal_stress: float32 [4096, 1024], P('strike', 'dip'), may hold values from 8 to 16
- direct_effect: float32 [4096, 1024], P('strike', 'dip'), may hold values from 0.01 to 0.04
- state_log: float32 [4096, 1024], P('strike', 'dip'), may hold values from 1 to 5
Outputs:
- next_rates: float32 [3, 4096, 1024], P(None, 'strike', 'dip')
- next_state: float32 [4096, 1024], P('strike', 'dip')
Inputs may be any that keep to these rules, and one draw needn't show every extreme that they name: `lengths`: how many of the newest slip-rate spectra enter each wavenumber's stress transfer.
All inputs are finite; a program needn't handle non-finite values.
Results may differ from a plain program's by a relative error of at most 0.0003.
Values sent between devices are 32-bit elements; how exact they have to be, the bound alone decides.
A program may use at most 128 MiB of HBM per device.

v0:
```python
import math

import jax
import jax.numpy as jnp
from jax import lax
from jax.sharding import PartitionSpec as P

HIST = 4
NEWTON = 2


time_step = 0.5
coupling = 0.5
decay_rate = 0.05
shear_speed = 0.6
opening_speed = 1.7
radiation = 0.5
healing = 1.0
slip_length = 2.0
highest = lax.Precision.HIGHEST


def area_sine(ratio):
    return jnp.log(ratio + jnp.sqrt(ratio * ratio + 1.0))


def wave_geometry(dip_modes, strike_modes, dip_cells, strike_cells):
    signed_dip = jnp.where(2 * dip_modes < dip_cells, dip_modes, dip_modes - dip_cells)
    signed_strike = jnp.where(
        2 * strike_modes < strike_cells, strike_modes, strike_modes - strike_cells
    )
    wave_dip = signed_dip.astype(jnp.float32) * (2.0 * math.pi / dip_cells)
    wave_strike = signed_strike.astype(jnp.float32) * (2.0 * math.pi / strike_cells)
    modulus = jnp.sqrt(wave_strike * wave_strike + wave_dip * wave_dip)
    anchor = (signed_dip == 0) & (signed_strike == 0)
    safe_modulus = jnp.where(anchor, 1.0, modulus)
    unit_strike = jnp.where(anchor, 1.0, wave_strike / safe_modulus)
    unit_dip = jnp.where(anchor, 0.0, wave_dip / safe_modulus)
    return (modulus, unit_strike, unit_dip)


def delay_mixing(geometry, delay):
    modulus, unit_strike, unit_dip = geometry
    phase_arg = modulus * (time_step * (delay + 1.0))
    envelope = -coupling * time_step * modulus * jnp.exp(-decay_rate * phase_arg)
    mode_two = envelope * jnp.cos(phase_arg)
    mode_three = envelope * jnp.cos(shear_speed * phase_arg)
    mode_one = envelope * jnp.cos(opening_speed * phase_arg)
    mix_along = unit_strike * unit_strike * mode_two + unit_dip * unit_dip * mode_three
    mix_cross = unit_strike * unit_dip * (mode_two - mode_three)
    mix_across = unit_dip * unit_dip * mode_two + unit_strike * unit_strike * mode_three
    return (mix_along, mix_cross, mix_across, mode_one)


def delay_term(spectrum, mixing, active):
    mix_along, mix_cross, mix_across, mode_one = mixing
    force_strike = (mix_along * spectrum[0] + mix_cross * spectrum[1]) * active
    force_dip = (mix_cross * spectrum[0] + mix_across * spectrum[1]) * active
    force_open = mode_one * spectrum[2] * active
    return jnp.stack([force_strike, force_dip, force_open])


def friction_step(force_field, prestress, normal_stress, direct_effect, state_log):
    load_strike = prestress[0] + force_field[0]
    load_dip = prestress[1] + force_field[1]
    traction = jnp.sqrt(load_strike * load_strike + load_dip * load_dip)
    strength = direct_effect * normal_stress
    factor = 2.0 * radiation * jnp.exp(-state_log)
    estimate = jnp.minimum(traction / strength, area_sine(traction / factor))
    for repeat in range(NEWTON):
        residual = traction - strength * estimate - factor * jnp.sinh(estimate)
        estimate = estimate + residual / (strength + factor * jnp.cosh(estimate))
    slip_speed = (traction - strength * estimate) / radiation
    unit_scale = slip_speed / jnp.maximum(traction, 1.0)
    new_rates = jnp.stack(
        [unit_scale * load_strike, unit_scale * load_dip, force_field[2] / radiation]
    )
    new_state = state_log + time_step * (healing * jnp.exp(-state_log) - slip_speed / slip_length)
    return (new_rates, new_state)


def phase_table(first_index, second_index, period):
    turn_count = first_index[:, None] * second_index[None, :] % period
    angle_table = turn_count.astype(jnp.float32) * (2.0 * math.pi / period)
    return (jnp.cos(angle_table), jnp.sin(angle_table))


def contract(pattern, first_operand, second_operand):
    return jnp.einsum(pattern, first_operand, second_operand, precision=highest)


def pair_section(part_real, part_imag, pattern, cos_table, sin_table, sign):
    out_real = contract(pattern, part_real, cos_table) - sign * contract(
        pattern, part_imag, sin_table
    )
    out_imag = contract(pattern, part_imag, cos_table) + sign * contract(
        pattern, part_real, sin_table
    )
    return (out_real, out_imag)


def twist_phase(part_real, part_imag, cos_table, sin_table, sign):
    out_real = cos_table * part_real - sign * sin_table * part_imag
    out_imag = cos_table * part_imag + sign * sin_table * part_real
    return (out_real, out_imag)


def shards(slip_rate, history, lengths, prestress, normal_stress, direct_effect, state_log):
    strike_count = lax.axis_size("strike")
    dip_count = lax.axis_size("dip")
    strike_index = lax.axis_index("strike")
    dip_index = lax.axis_index("dip")
    row_count = slip_rate.shape[1]
    dip_block = slip_rate.shape[2]
    mode_rows = history.shape[3]
    strike_cells = history.shape[4]
    dip_cells = dip_block * dip_count
    unit_modes = dip_count * mode_rows
    quarter_rows = row_count // dip_count
    norm_dip = 1.0 / math.sqrt(dip_cells)
    norm_strike = 1.0 / math.sqrt(strike_cells)
    local_modes = jnp.arange(mode_rows, dtype=jnp.int32)
    dip_modes = (strike_index * dip_count + dip_index) * mode_rows + local_modes
    strike_modes = jnp.arange(strike_cells, dtype=jnp.int32)
    geometry = wave_geometry(dip_modes[:, None], strike_modes[None, :], dip_cells, strike_cells)
    coarse_all = jnp.arange(unit_modes, dtype=jnp.int32)
    coarse_own = dip_index * mode_rows + local_modes
    outer_index = jnp.arange(strike_count, dtype=jnp.int32)
    inner_index = jnp.arange(row_count, dtype=jnp.int32)
    cos_outer, sin_outer = phase_table(outer_index, outer_index, strike_count)
    cos_bend, sin_bend = phase_table(outer_index, inner_index, strike_cells)
    cos_bend = cos_bend * norm_strike
    sin_bend = sin_bend * norm_strike
    cos_inner, sin_inner = phase_table(inner_index, inner_index, row_count)

    def strike_forward(spectral):
        item_count = spectral.shape[0]
        grid_view = spectral.reshape(item_count, 2, mode_rows, strike_count, row_count)
        section_real, section_imag = pair_section(
            grid_view[:, 0], grid_view[:, 1], "ngpr,kp->ngkr", cos_outer, sin_outer, -1.0
        )
        bent_real, bent_imag = twist_phase(section_real, section_imag, cos_bend, sin_bend, -1.0)
        out_real, out_imag = pair_section(
            bent_real, bent_imag, "ngkr,rm->ngmk", cos_inner, sin_inner, -1.0
        )
        return jnp.stack([out_real, out_imag], axis=1).reshape(
            item_count, 2, mode_rows, strike_cells
        )

    def strike_inverse(spectral):
        grid_view = spectral.reshape(3, 2, mode_rows, row_count, strike_count)
        section_real, section_imag = pair_section(
            grid_view[:, 0], grid_view[:, 1], "ngmk,rm->ngrk", cos_inner, sin_inner, 1.0
        )
        bent_real, bent_imag = twist_phase(section_real, section_imag, cos_bend.T, sin_bend.T, 1.0)
        out_real, out_imag = pair_section(
            bent_real, bent_imag, "ngrk,kp->ngpr", cos_outer, sin_outer, 1.0
        )
        return jnp.stack([out_real, out_imag], axis=1).reshape(3, 2, mode_rows, strike_cells)

    def to_modes(space_field):
        gathered = lax.all_gather(space_field, "dip", axis=2, tiled=True)
        cos_first, sin_first = phase_table(coarse_all, coarse_own, unit_modes)
        cos_twist, sin_twist = phase_table(outer_index, coarse_own, dip_cells)
        grid_view = gathered.reshape(3, row_count, unit_modes, strike_count)
        first_real = contract("cxab,au->cxbu", grid_view, cos_first)
        first_imag = -contract("cxab,au->cxbu", grid_view, sin_first)
        bent_real, bent_imag = twist_phase(
            first_real, first_imag, cos_twist * norm_dip, sin_twist * norm_dip, -1.0
        )
        out_real, out_imag = pair_section(
            bent_real, bent_imag, "cxbi,bs->csix", cos_outer, sin_outer, -1.0
        )
        dip_spec = jnp.stack([out_real, out_imag], axis=1).reshape(3, 2, dip_block, row_count)
        return strike_forward(
            lax.all_to_all(dip_spec, "strike", split_axis=2, concat_axis=3, tiled=True)
        )

    def to_space(mode_field):
        mixed_rows = strike_inverse(mode_field)
        sectioned = mixed_rows.reshape(3, 2, mode_rows, strike_count, dip_count * quarter_rows)
        back = lax.all_to_all(
            lax.all_to_all(sectioned, "strike", split_axis=3, concat_axis=2, tiled=True),
            "dip",
            split_axis=4,
            concat_axis=2,
            tiled=True,
        )
        grid_view = back.reshape(3, 2, dip_count, strike_count, mode_rows, quarter_rows)
        cos_last, sin_last = phase_table(coarse_all, coarse_all, unit_modes)
        first_real, first_imag = pair_section(
            grid_view[:, 0], grid_view[:, 1], "cdsix,bs->cxbdi", cos_outer, sin_outer, 1.0
        )
        first_real = first_real.reshape(3, quarter_rows, strike_count, unit_modes)
        first_imag = first_imag.reshape(3, quarter_rows, strike_count, unit_modes)
        cos_twist, sin_twist = phase_table(outer_index, coarse_all, dip_cells)
        bent_real, bent_imag = twist_phase(
            first_real, first_imag, cos_twist * norm_dip, sin_twist * norm_dip, 1.0
        )
        space_part = contract("cxbu,au->cxab", bent_real, cos_last) - contract(
            "cxbu,au->cxab", bent_imag, sin_last
        )
        space_rows = space_part.reshape(3, quarter_rows, dip_cells)
        return lax.all_to_all(space_rows, "dip", split_axis=2, concat_axis=1, tiled=True)

    def transfer(recent):
        recent_count = len(recent)
        summed = jnp.zeros(recent[0].shape, jnp.float32)
        for offset in range(HIST):
            if offset < recent_count:
                source = recent[offset]
            else:
                source = history[offset - recent_count].astype(jnp.float32)
            active = (offset < lengths).astype(jnp.float32)
            summed = summed + delay_term(source, delay_mixing(geometry, float(offset)), active)
        return summed

    first_spec = to_modes(slip_rate)
    force_field = to_space(transfer([first_spec]))
    next_rates, next_state = friction_step(
        force_field, prestress, normal_stress, direct_effect, state_log
    )
    second_spec = to_modes(next_rates)
    force_field = to_space(transfer([second_spec, first_spec]))
    next_rates, next_state = friction_step(
        force_field, prestress, normal_stress, direct_effect, next_state
    )
    return (next_rates, next_state)


def solution(mesh):
    return jax.shard_map(
        shards,
        mesh=mesh,
        in_specs=(
            P(None, "strike", "dip"),
            P(None, None, None, ("strike", "dip"), None),
            P(("strike", "dip"), None),
            P(None, "strike", "dip"),
            P("strike", "dip"),
            P("strike", "dip"),
            P("strike", "dip"),
        ),
        out_specs=(P(None, "strike", "dip"), P("strike", "dip")),
        check_vma=False,
    )
```

profile of v0, /device:TPU:0, one launch (start us, length us, event | category | flops | bytes accessed | tf_op | source)
XLA Modules:
  0.0 915.7 jit_solution(3905725277316915255)
XLA Ops:
  10.4 18.0 %multiply_add_fusion.8 = (f32[32,4096]{1,0:T(8,128)}, f32[32,4096]{1,0:T(8,128)}, f32[32,4096]{1,0:T(8,128)}, f32[32,4096]{1,0:T(8,128)}, f32[32,4096]{1,0:T(8,1...) fusion(f32[32]{0:T(128)S(1)} %get-tuple-element.95, ...), kind=kLoop, calls=%fused_computation.286 | loop fusion | flops 7602176 | bytes 6328608 | tf_op jit(solution)/shard_map/add | solution.py:49
  28.4 31.1 %all-gather.3.cloned.1.call-done = f32[3,512,1024]{1,2,0:T(8,128)} async-done(((f32[3,512,256]{1,2,0:T(8,128)}), f32[3,512,1024]{1,2,0:T(8,128)}) %all-gather.3.cloned.1.call-update) | async-done | bytes 6291472 | tf_op jit(solution)/shard_map/all_gather | solution.py:162
  59.5 6.6 copy.529
  66.1 9.1 fusion.183
  75.2 6.5 fusion.4
  93.2 4.1 copy.541
  97.3 5.9 all-to-all-start
  108.6 5.1 slice_convert_fusion
  131.9 3.8 copy.553
  135.7 5.8 add_multiply_fusion.9
  170.8 3.9 copy.555
  187.7 12.2 %multiply_add_fusion.5 = (f32[32,512,8]{1,0,2:T(8,128)S(1)}, f32[32,512,8]{1,0,2:T(8,128)}, f32[32,512,8]{1,0,2:T(8,128)S(1)}, f32[32,512,8]{1,0,2:T(8,128)S(1)}...) fusion(f32[32]{0:T(128)S(1)} %get-tuple-element.95, ...), kind=kLoop, calls=%fused_computation.268 | loop fusion | flops 5505024 | bytes 4231456 | tf_op jit(solution)/shard_map/add | solution.py:51
  199.9 4.4 copy.767
  210.8 7.2 fusion.66
  218.0 7.0 fusion.62
  225.0 7.5 subtract_bitcast_fusion.9
  232.6 7.3 add_bitcast_fusion.7
  247.6 6.5 fusion.33
  254.1 6.9 fusion.32
  261.0 6.6 convolution_add_fusion.3
  267.6 7.1 subtract_bitcast_fusion.8
  286.6 76.4 %all_to_all.126 = f32[3,2,32,8,512]{4,2,0,1,3:T(8,128)S(1)} all-to-all(f32[3,2,32,8,512]{4,2,0,1,3:T(8,128)S(1)} %copy.576), channel_id=1, replica_groups=mesh['strike'=8,'dip'=4] {'strike'}, dimensions={3} | all-to-all | bytes 6291456 | tf_op jit(solution)/shard_map/all_to_all | solution.py:183
  370.5 36.8 %all-to-all-done.2 = f32[3,2,256,1,512]{2,1,0,3,4:T(2,128)S(1)} async-done(((f32[3,2,256,1,512]{2,1,0,3,4:T(2,128)}), f32[3,2,256,1,512]{2,1,0,3,4:T(2,128)S(1)}, u32[]{:S(2)}, u32[]{:S(2)}) %all-to-all-start.2) | async-done | bytes 3145760 | tf_op jit(solution)/shard_map/all_to_all | solution.py:182
  430.0 28.2 %all_to_all.127 = f32[3,128,1024]{1,0,2:T(4,128)S(1)} all-to-all(f32[3,128,1024]{1,0,2:T(4,128)S(1)} %copy.588), channel_id=1, replica_groups=mesh['strike'=8,'dip'=4] {'dip'}, dimensions={2} | all-to-all | bytes 3145728 | tf_op jit(solution)/shard_map/all_to_all | solution.py:204
  461.8 3.8 multiply_bitcast_fusion.3
  467.9 44.6 %all-gather.5.cloned.1.call-done = f32[3,512,1024]{2,1,0:T(8,128)} async-done(((f32[3,512,256]{2,1,0:T(8,128)}), f32[3,512,1024]{2,1,0:T(8,128)}) %all-gather.5.cloned.1.call-update) | async-done | bytes 6291472 | tf_op jit(solution)/shard_map/all_gather | solution.py:162
  512.5 6.5 copy.593
  519.1 6.6 copy.594
  525.7 9.3 %fusion.181 = f32[3,512,8,32]{1,3,2,0:T(8,128)S(1)} fusion(f32[3,512,128,8]{2,1,3,0:T(8,128)} %copy.594, s32[32]{0:T(128)S(1)} %iota_add_fusion.1), kind=kOutput, calls=%fused_computation.361 | convolution fusion | flops 604037120 | bytes 7864448 | tf_op jit(solution)/shard_map/cxab,au->cxbu/dot_general | solution.py:89
  534.9 6.8 multiply_subtract_fusion.1
  553.3 4.1 copy.606
  557.3 5.6 all-to-all-start.4
  585.0 3.7 copy.626
  597.8 3.7 copy.624
  601.5 32.7 %all-to-all-done.4 = f32[3,2,256,512]{3,1,0,2:T(2,128)} async-done(((f32[3,2,256,512]{3,1,0,2:T(2,128)}), f32[3,2,256,512]{3,1,0,2:T(2,128)}, u32[]{:S(2)}, u32[]{:S(2)}) %all-to-all-start.4) | async-done | bytes 3145760 | tf_op jit(solution)/shard_map/all_to_all | solution.py:176
  634.2 3.7 copy.766
  644.4 7.2 fusion.48
  651.6 7.0 fusion.44
  658.6 7.6 subtract_bitcast_fusion.3
  666.2 7.3 add_bitcast_fusion.2
  678.5 6.5 fusion.37
  685.0 6.9 fusion.36
  691.9 6.6 convolution_add_fusion.2
  698.5 7.1 subtract_bitcast_fusion.2
  717.3 74.3 %all_to_all.128 = f32[3,2,32,8,512]{4,2,0,1,3:T(8,128)S(1)} all-to-all(f32[3,2,32,8,512]{4,2,0,1,3:T(8,128)S(1)} %copy.635), channel_id=1, replica_groups=mesh['strike'=8,'dip'=4] {'strike'}, dimensions={3} | all-to-all | bytes 6291456 | tf_op jit(solution)/shard_map/all_to_all | solution.py:183
  793.5 5.9 copy.637
  799.3 40.6 %all_to_all.129 = f32[3,2,256,1,512]{2,1,0,3,4:T(2,128)S(1)} all-to-all(f32[3,2,256,1,512]{2,1,0,3,4:T(2,128)} %copy.637), channel_id=1, replica_groups=mesh['strike'=8,'dip'=4] {'dip'}, dimensions={4} | all-to-all | bytes 6291456 | tf_op jit(solution)/shard_map/all_to_all | solution.py:182
  871.0 28.2 %all_to_all.130 = f32[3,128,1024]{1,0,2:T(4,128)S(1)} all-to-all(f32[3,128,1024]{1,0,2:T(4,128)S(1)} %copy.647), channel_id=1, replica_groups=mesh['strike'=8,'dip'=4] {'dip'}, dimensions={2} | all-to-all | bytes 3145728 | tf_op jit(solution)/shard_map/all_to_all | solution.py:204
  (252 shorter events, 250.1 us)
Async XLA Ops:
  7.2 52.3 %all-gather.3.cloned.1.call-start = ((), (), s32[]{:S(2)}) async-start(), calls=%async_computation.8 | async-start | bytes 7864320 | tf_op jit(solution)/shard_map/all_gather | solution.py:162
  66.1 9.1 copy-start.1
  97.3 5.9 copy-start.58
  97.3 102.6 %all-to-all-start = ((f32[3,2,256,512]{3,1,0,2:T(2,128)}), f32[3,2,256,512]{3,1,0,2:T(2,128)}, u32[]{:S(2)}, u32[]{:S(2)}) async-start(f32[3,2,256,512]{3,1,0,2:T(2,128)} %copy.541), calls=%async_computation | async-start | bytes 6291456 | tf_op jit(solution)/shard_map/all_to_all | solution.py:176
  108.6 5.2 copy-start.53
  108.6 5.2 copy-start.54
  108.6 5.2 copy-start.55
  108.6 5.2 copy-start.56
  108.6 5.2 copy-start.57
  113.8 3.6 copy-start.2
  131.9 3.8 copy-start.3
  145.2 3.7 copy-start.43
  151.6 3.7 copy-start.41
  158.0 3.7 copy-start.19
  164.4 3.7 copy-start.18
  170.8 3.9 copy-start.45
  177.4 3.7 copy-start.44
  199.8 40.1 %copy-start.14 = (f32[32,512,8]{1,0,2:T(8,128)}, f32[32,512,8]{1,0,2:T(8,128)S(1)}, u32[]{:S(2)}) copy-start(f32[32,512,8]{1,0,2:T(8,128)S(1)} %get-tuple-element.87) | copy-start | bytes 1572868
  199.8 42.4 %copy-start.8 = (f32[32,512,8]{1,0,2:T(8,128)}, f32[32,512,8]{1,0,2:T(8,128)S(1)}, u32[]{:S(2)}) copy-start(f32[32,512,8]{1,0,2:T(8,128)S(1)} %get-tuple-element.74) | copy-start | bytes 1572868
  199.9 42.4 %copy-start.10 = (f32[32,512,8]{1,0,2:T(8,128)}, f32[32,512,8]{1,0,2:T(8,128)S(1)}, u32[]{:S(2)}) copy-start(f32[32,512,8]{1,0,2:T(8,128)S(1)} %get-tuple-element.75) | copy-start | bytes 1572868
  199.9 42.4 %copy-start.12 = (f32[32,512,8]{1,0,2:T(8,128)}, f32[32,512,8]{1,0,2:T(8,128)S(1)}, u32[]{:S(2)}) copy-start(f32[32,512,8]{1,0,2:T(8,128)S(1)} %get-tuple-element.77) | copy-start | bytes 1572868
  232.5 7.4 copy-start.6
  232.5 7.4 copy-start.16
  232.6 7.4 copy-start.50
  232.6 7.4 copy-start.51
  239.9 4.1 copy-start.35
  242.3 3.1 copy-start.32
  242.3 3.4 copy-start.33
  242.3 3.7 copy-start.34
  366.7 40.6 %all-to-all-start.2 = ((f32[3,2,256,1,512]{2,1,0,3,4:T(2,128)}), f32[3,2,256,1,512]{2,1,0,3,4:T(2,128)S(1)}, u32[]{:S(2)}, u32[]{:S(2)}) async-start(f32[3,2,256,1,512]{2,1,0,3,4:T(2,128)} %copy.578), calls=%async_computation.2 | async-start | bytes 6291456 | tf_op jit(solution)/shard_map/all_to_all | solution.py:182
  370.4 142.1 %all-gather.5.cloned.1.call-start = ((), (), s32[]{:S(2)}) async-start(), calls=%async_computation.9 | async-start | bytes 7864320 | tf_op jit(solution)/shard_map/all_gather | solution.py:162
  525.7 9.3 %copy-start = (f32[3,512,128,8]{2,1,3,0:T(8,128)S(1)}, f32[3,512,128,8]{2,1,3,0:T(8,128)}, u32[]{:S(2)}) copy-start(f32[3,512,128,8]{2,1,3,0:T(8,128)} %copy.594) | copy-start | bytes 18874372
  557.3 5.7 copy-start.22
  557.3 76.9 %all-to-all-start.4 = ((f32[3,2,256,512]{3,1,0,2:T(2,128)}), f32[3,2,256,512]{3,1,0,2:T(2,128)}, u32[]{:S(2)}, u32[]{:S(2)}) async-start(f32[3,2,256,512]{3,1,0,2:T(2,128)} %copy.606), calls=%async_computation.4 | async-start | bytes 6291456 | tf_op jit(solution)/shard_map/all_to_all | solution.py:176
  565.7 3.7 copy-start.21
  572.1 3.7 copy-start.20
  578.6 3.7 copy-start.25
  585.0 3.7 copy-start.24
  591.4 3.7 copy-start.23
  666.2 7.3 copy-start.7
  666.2 7.3 copy-start.9
  666.2 7.3 copy-start.11
  666.2 7.3 copy-start.13
  666.2 7.3 copy-start.15
  666.2 8.4 copy-start.47
  673.6 3.1 copy-start.42
  673.6 3.3 copy-start.46
  863.6 3.6 copy-start.5
  (16 other events, 32.7 us)
Sparse Core Ops, SparseCore 0:
  10.4 49.0 all-gather.2
  468.0 44.4 all-gather.4
where the time goes:
time: 922 us; the launch traced here: 916 us
  blocking collectives  248 us (27%)
  matrix products  223 us (24%)
  local copies, waits for them, and re-layouts  196 us (21%)
  waiting for transfers between devices  145 us (16%)
  other arithmetic  72.2 us (8%)
  between operations  15.7 us (2%)
  starting transfers between devices  15.3 us (2%)
    dot_general x56, matrix products, contract(): return jnp.einsum(pattern, first_operand, second_operand, precision=highest)  223 us
    all_to_all x2, blocking collectives, to_space(): lax.all_to_all(sectioned, 'strike', split_axis=3, concat_axis=2, tiled=True)  151 us
    all_gather x2, waiting for transfers between devices, to_modes(): gathered = lax.all_gather(space_field, 'dip', axis=2, tiled=True)  75.7 us
    all_to_all x2, blocking collectives, to_space(): lax.all_to_all(space_rows, 'dip', split_axis=2, concat_axis=1, tiled=True)  56.3 us
    another operation x15, local copies, waits for them, and re-layouts, delay_term(): return jnp.stack([force_strike, force_dip, force_open])  55.6 us
    all_to_all x1, blocking collectives, to_space(): lax.all_to_all(lax.all_to_all(sectioned, 'strike', split_axis=3, concat_a...  40.6 us
    all_to_all x1, waiting for transfers between devices, to_space(): lax.all_to_all(lax.all_to_all(sectioned, 'strike', split_axis=3, concat_a...  36.8 us
    all_to_all x2, waiting for transfers between devices, to_modes(): lax.all_to_all(dip_spec, 'strike', split_axis=2, concat_axis=3, tiled=True)  32.7 us
  transfers between devices with their start and end apart: 5, of which 4 were waited for; matrix products, arithmetic and copies ran while one was open for 17% of the time, Pallas kernels for 0%

commit v1 on v0

--- a/solution.py
+++ b/solution.py
@@ -1,8 +1,12 @@
+import functools
 import math
 
 import jax
 import jax.numpy as jnp
+import numpy as np
 from jax import lax
+from jax.experimental import pallas as pl
+from jax.experimental.pallas import tpu as pltpu
 from jax.sharding import PartitionSpec as P
 
 HIST = 4
@@ -228,9 +232,289 @@
     return (next_rates, next_state)
 
 
+LANES = 128
+SUBLANES = 8
+
+
+def turn(part_real, part_imag, count, index, sign):
+    index = index % count
+    if index == 0:
+        return part_real, part_imag
+    if 2 * index == count:
+        return -part_real, -part_imag
+    if 4 * index == count:
+        return (-part_imag, part_real) if sign > 0 else (part_imag, -part_real)
+    angle = sign * 2.0 * math.pi * index / count
+    cosine, sine = math.cos(angle), math.sin(angle)
+    if 8 * index == count:
+        return (
+            cosine * (part_real - part_imag) if sign > 0 else cosine * (part_real + part_imag),
+            cosine * (part_imag + part_real) if sign > 0 else cosine * (part_imag - part_real),
+        )
+    return (
+        cosine * part_real - sine * part_imag,
+        cosine * part_imag + sine * part_real,
+    )
+
+
+def butterfly(reals, imags, sign):
+    count = len(reals)
+    if count == 1:
+        return reals, imags
+    even_real, even_imag = butterfly(reals[0::2], imags[0::2], sign)
+    odd_real, odd_imag = butterfly(reals[1::2], imags[1::2], sign)
+    top, low = [], []
+    for index in range(count // 2):
+        bent_real, bent_imag = turn(odd_real[index], odd_imag[index], count, index, sign)
+        top.append((even_real[index] + bent_real, even_imag[index] + bent_imag))
+        low.append((even_real[index] - bent_real, even_imag[index] - bent_imag))
+    both = top + low
+    return [item[0] for item in both], [item[1] for item in both]
+
+
+def split_product(left, high, low):
+    left_high = left.astype(jnp.bfloat16)
+    left_low = (left - left_high.astype(jnp.float32)).astype(jnp.bfloat16)
+    dot = functools.partial(jnp.dot, preferred_element_type=jnp.float32)
+    return dot(left_high, high) + (dot(left_low, high) + dot(left_high, low))
+
+
+def owner_kernel(keep, *refs):
+    if keep:
+        x_ref, mix_ref, add_ref, later_mix_ref, later_ref, bend_ref, high_ref, low_ref = refs[:8]
+        out_ref, later_out_ref, line, spec = refs[8:]
+    else:
+        x_ref, mix_ref, add_ref, bend_ref, high_ref, low_ref = refs[:6]
+        out_ref, line, spec = refs[6:]
+    blocks = x_ref.shape[0]
+    rows = blocks * SUBLANES
+    width = 2 * LANES
+    halves = (slice(0, LANES), slice(LANES, width))
+    for comp in range(3):
+        own = slice(comp * LANES, (comp + 1) * LANES)
+        reals, imags = butterfly(
+            [x_ref[block, 0, :, own] for block in range(blocks)],
+            [x_ref[block, 1, :, own] for block in range(blocks)],
+            -1,
+        )
+        for mode in range(blocks):
+            cosine = bend_ref[0, pl.ds(mode, 1), :]
+            sine = bend_ref[1, pl.ds(mode, 1), :]
+            line[comp, mode, :, halves[0]] = reals[mode] * cosine + imags[mode] * sine
+            line[comp, mode, :, halves[1]] = imags[mode] * cosine - reals[mode] * sine
+        spec[comp] = split_product(
+            line[comp].reshape(rows, width), high_ref[0], low_ref[0]
+        ).reshape(blocks, SUBLANES, width)
+    for half in halves:
+        along, across, opening = (spec[comp, :, :, half] for comp in range(3))
+        line[0, :, :, half] = mix_ref[0] * along + mix_ref[1] * across + add_ref[0, :, :, half]
+        line[1, :, :, half] = mix_ref[1] * along + mix_ref[2] * across + add_ref[1, :, :, half]
+        line[2, :, :, half] = mix_ref[3] * opening + add_ref[2, :, :, half]
+        if keep:
+            later_out_ref[0, :, :, half] = (
+                later_mix_ref[0] * along + later_mix_ref[1] * across + later_ref[0, :, :, half]
+            )
+            later_out_ref[1, :, :, half] = (
+                later_mix_ref[1] * along + later_mix_ref[2] * across + later_ref[1, :, :, half]
+            )
+            later_out_ref[2, :, :, half] = later_mix_ref[3] * opening + later_ref[2, :, :, half]
+    for comp in range(3):
+        own = slice(comp * LANES, (comp + 1) * LANES)
+        spec[comp] = split_product(
+            line[comp].reshape(rows, width), high_ref[1], low_ref[1]
+        ).reshape(blocks, SUBLANES, width)
+        reals, imags = [], []
+        for mode in range(blocks):
+            cosine = bend_ref[0, pl.ds(mode, 1), :]
+            sine = bend_ref[1, pl.ds(mode, 1), :]
+            real, imag = spec[comp, mode, :, halves[0]], spec[comp, mode, :, halves[1]]
+            reals.append(real * cosine - imag * sine)
+            imags.append(imag * cosine + real * sine)
+        reals, imags = butterfly(reals, imags, 1)
+        for block in range(blocks):
+            out_ref[block, 0, :, own] = reals[block]
+            out_ref[block, 1, :, own] = imags[block]
+
+
+def strike_pass(arrived, mixing, addend, tables, later=None):
+    blocks, _, modes, depth = arrived.shape
+    bend, high, low = tables
+    tiles = modes // SUBLANES
+    wide = pl.BlockSpec((blocks, 2, SUBLANES, depth), lambda tile: (0, 0, tile, 0))
+    factors = pl.BlockSpec((4, blocks, SUBLANES, LANES), lambda tile: (0, 0, tile, 0))
+    field = pl.BlockSpec((3, blocks, SUBLANES, 2 * LANES), lambda tile: (0, 0, tile, 0))
+    fixed = [
+        pl.BlockSpec(item.shape, lambda tile, rank=item.ndim: (0,) * rank) for item in tables
+    ]
+    operands = [arrived, mixing, addend]
+    in_specs = [wide, factors, field]
+    out_specs = [wide]
+    out_shape = [jax.ShapeDtypeStruct(arrived.shape, jnp.float32)]
+    if later is not None:
+        operands += list(later)
+        in_specs += [factors, field]
+        out_specs.append(field)
+        out_shape.append(jax.ShapeDtypeStruct(addend.shape, jnp.float32))
+    return pl.pallas_call(
+        functools.partial(owner_kernel, later is not None),
+        grid=(tiles,),
+        in_specs=in_specs + fixed,
+        out_specs=out_specs,
+        out_shape=out_shape,
+        scratch_shapes=[
+            pltpu.VMEM((3, blocks, SUBLANES, 2 * LANES), jnp.float32),
+            pltpu.VMEM((3, blocks, SUBLANES, 2 * LANES), jnp.float32),
+        ],
+        compiler_params=pltpu.CompilerParams(vmem_limit_bytes=40 * 1024 * 1024),
+        cost_estimate=pl.CostEstimate(
+            flops=12 * arrived.size * 2 * LANES, bytes_accessed=16 * arrived.size, transcendentals=0
+        ),
+    )(*operands, bend, high, low)
+
+
+def halves_of(table):
+    table = table.astype(np.float32)
+    high = table.astype(jnp.bfloat16)
+    return high, (table - high.astype(np.float32)).astype(jnp.bfloat16)
+
+
+def strike_tables(blocks, strike_cells):
+    first, second = np.arange(blocks)[:, None], np.arange(LANES)[None, :]
+    angle = 2.0 * np.pi * (first * second % strike_cells) / strike_cells
+    bend = np.stack([np.cos(angle), np.sin(angle)]) / math.sqrt(strike_cells)
+    line = np.arange(LANES)
+    angle = 2.0 * np.pi * (line[:, None] * line[None, :] % LANES) / LANES
+    cosine, sine = np.cos(angle), np.sin(angle)
+    forward = np.block([[cosine, -sine], [sine, cosine]])
+    inverse = np.block([[cosine, sine], [-sine, cosine]])
+    high, low = halves_of(np.stack([forward, inverse]))
+    return jnp.asarray(bend, jnp.float32), jnp.asarray(high), jnp.asarray(low)
+
+
+def dip_table(devices, dip_cells):
+    modes = np.arange(dip_cells)
+    angle = 2.0 * np.pi * (modes[:, None] * modes[None, :] % dip_cells) / dip_cells
+    pair = np.stack([np.cos(angle), -np.sin(angle)]) / math.sqrt(dip_cells)
+    pair = pair.reshape(2, devices, dip_cells // devices, dip_cells).transpose(1, 0, 2, 3)
+    return jnp.asarray(pair.reshape(2 * dip_cells, dip_cells), jnp.float32)
+
+
+def all_mixing(geometry):
+    modulus, unit_strike, unit_dip = geometry
+    base = modulus * time_step
+    decay = jnp.exp(-decay_rate * base)
+    speeds = (1.0, shear_speed, opening_speed)
+    one = [jnp.cos(speed * base) for speed in speeds]
+    last, now = [1.0, 1.0, 1.0], list(one)
+    envelope = -coupling * time_step * modulus
+    square_strike, square_dip = unit_strike * unit_strike, unit_dip * unit_dip
+    cross = unit_strike * unit_dip
+    factors = []
+    for _ in range(HIST):
+        envelope = envelope * decay
+        two, three, opening = (envelope * value for value in now)
+        factors.append(
+            (
+                square_strike * two + square_dip * three,
+                cross * (two - three),
+                square_dip * two + square_strike * three,
+                opening,
+            )
+        )
+        last, now = now, [2.0 * a * b - c for a, b, c in zip(one, now, last)]
+    return factors
+
+
+def fast_shards(slip_rate, history, lengths, prestress, normal_stress, direct_effect, state_log):
+    strike_count = lax.axis_size("strike")
+    dip_count = lax.axis_size("dip")
+    devices = strike_count * dip_count
+    row_count = slip_rate.shape[1]
+    dip_cells = slip_rate.shape[2] * dip_count
+    modes = history.shape[3]
+    strike_cells = history.shape[4]
+    rows = row_count // dip_count
+    own = lax.axis_index("strike") * dip_count + lax.axis_index("dip")
+    table = dip_table(devices, dip_cells)
+    tables = strike_tables(devices, strike_cells)
+    local_modes = own * modes + jnp.arange(modes, dtype=jnp.int32)
+    strike_modes = jnp.arange(strike_cells, dtype=jnp.int32)
+    precise = lax.Precision.HIGH
+
+    def send(space_field):
+        spread = lax.all_to_all(space_field, "dip", split_axis=1, concat_axis=2, tiled=True)
+        dip_spec = jnp.einsum(
+            "kz,xz->kx", table, spread.reshape(3 * rows, dip_cells), precision=precise
+        )
+        moved = lax.all_to_all(
+            dip_spec, ("strike", "dip"), split_axis=0, concat_axis=0, tiled=True
+        )
+        return moved.reshape(devices, 2, modes, 3 * rows)
+
+    def receive(strike_rows):
+        moved = lax.all_to_all(
+            strike_rows.reshape(2 * dip_cells, 3 * rows),
+            ("strike", "dip"),
+            split_axis=0,
+            concat_axis=0,
+            tiled=True,
+        )
+        space_rows = jnp.einsum("kx,kz->xz", moved, table, precision=precise)
+        return lax.all_to_all(
+            space_rows.reshape(3, rows, dip_cells), "dip", split_axis=2, concat_axis=1, tiled=True
+        )
+
+    def by_residue(plain):
+        lead = plain.shape[:-1]
+        return plain.reshape(lead + (rows, devices))
+
+    residue = jnp.arange(devices, dtype=jnp.int32)[:, None, None]
+    step = jnp.arange(rows, dtype=jnp.int32)[None, None, :]
+    sorted_mixing = all_mixing(
+        wave_geometry(local_modes[None, :, None], residue + devices * step, dip_cells, strike_cells)
+    )
+    reach = jnp.transpose(by_residue(lengths), (2, 0, 1))
+    mixing = jnp.stack(sorted_mixing[0])
+    later_mixing = jnp.stack(sorted_mixing[1]) * (1 < reach).astype(jnp.float32)
+    plain_mixing = all_mixing(
+        wave_geometry(local_modes[:, None], strike_modes[None, :], dip_cells, strike_cells)
+    )
+
+    def past(first):
+        summed = 0.0
+        for offset in range(first, HIST):
+            active = (offset < lengths).astype(jnp.float32)
+            source = history[offset - first].astype(jnp.float32)
+            summed = summed + delay_term(source, plain_mixing[offset], active)
+        summed = jnp.transpose(by_residue(summed), (0, 4, 2, 1, 3))
+        return summed.reshape(3, devices, modes, 2 * rows)
+
+    arrived = send(slip_rate)
+    strike_rows, addend = strike_pass(
+        arrived, mixing, past(1), tables, (later_mixing, past(2))
+    )
+    next_rates, next_state = friction_step(
+        receive(strike_rows), prestress, normal_stress, direct_effect, state_log
+    )
+    (strike_rows,) = strike_pass(send(next_rates), mixing, addend, tables)
+    return friction_step(
+        receive(strike_rows), prestress, normal_stress, direct_effect, next_state
+    )
+
+
+def choose(slip_rate, history, *others):
+    devices = lax.axis_size("strike") * lax.axis_size("dip")
+    fits = (
+        history.shape[4] == devices * LANES
+        and history.shape[3] % SUBLANES == 0
+        and devices & (devices - 1) == 0
+    )
+    return (fast_shards if fits else shards)(slip_rate, history, *others)
+
+
 def solution(mesh):
     return jax.shard_map(
-        shards,
+        choose,
         mesh=mesh,
         in_specs=(
             P(None, "strike", "dip"),

time: 922 us -> 619 us (0.67)
  matrix products: 223 us -> 39.5 us
  waiting for transfers between devices: 145 us -> 13.6 us
  blocking collectives: 248 us -> 314 us
  local copies, waits for them, and re-layouts: 196 us -> 163 us
  other arithmetic: 72.2 us -> 55.9 us
  between operations: 15.7 us -> 1.29 us
  Pallas kernels: 0 us -> 12.9 us
    dot_general x56 -> x4, matrix products: 223 us -> 39.5 us  [the longest x2 22.1 us: receive(): space_rows = jnp.einsum('kx,kz->xz', moved, table, precision=precise)]
    all_gather x2 -> x0, waiting for transfers between devices: 75.7 us -> none  [to_modes(): gathered = lax.all_gather(space_field, 'dip', axis=2, tiled=True)]
    all_to_all x5 -> x6, blocking collectives: 248 us -> 314 us  [the longest x2 152 us: receive(): lax.all_to_all(strike_rows.reshape(2 * dip_cells, 3 * rows), ('strike', '...]
    all_to_all x3 -> x2, waiting for transfers between devices: 69.5 us -> 13.6 us  [the longest x1 13.6 us: send(): lax.all_to_all(space_field, 'dip', split_axis=1, concat_axis=2, tiled=True)]
    another operation x15 -> x30, local copies, waits for them, and re-layouts: 55.6 us -> 110 us  [delay_term(): return jnp.stack([force_strike, force_dip, force_open])]
    mul x18 -> x0, local copies, waits for them, and re-layouts: 47.2 us -> none  [the longest x8 20.1 us: delay_term(): force_strike = (mix_along * spectrum[0] + mix_cross * spectrum[1]) * active]
    add x5 -> x2, other arithmetic: 33.2 us -> 14.8 us  [all_mixing(): square_strike * two + square_dip * three]
    all_to_all x12 -> x6, local copies, waits for them, and re-layouts: 29.8 us -> 15.4 us  [the longest x2 6 us: receive(): lax.all_to_all(strike_rows.reshape(2 * dip_cells, 3 * rows), ('strike', '...]
  transfers between devices with their start and end apart: 5 -> 2, of which waited for: 4 -> 1; matrix products, arithmetic and copies ran while one was open for 17% -> 29% of each run, Pallas kernels for 0% -> 0%
where the time goes in v1:
time: 619 us; the launch traced here: 610 us
  blocking collectives  314 us (51%)
  local copies, waits for them, and re-layouts  163 us (26%)
  other arithmetic  55.9 us (9%)
  matrix products  39.5 us (6%)
  waiting for transfers between devices  13.6 us (2%)
  Pallas kernels  12.9 us (2%)
  starting transfers between devices  10.6 us (2%)
    all_to_all x2, blocking collectives, receive(): lax.all_to_all(strike_rows.reshape(2 * dip_cells, 3 * rows), ('strike', '...  152 us
    another operation x30, local copies, waits for them, and re-layouts, delay_term(): return jnp.stack([force_strike, force_dip, force_open])  110 us
    all_to_all x1, blocking collectives, send(): lax.all_to_all(dip_spec, ('strike', 'dip'), split_axis=0, concat_axis=0,...  73.8 us
    all_to_all x2, blocking collectives, receive(): lax.all_to_all(space_rows.reshape(3, rows, dip_cells), 'dip', split_axis=...  59.1 us
    all_to_all x1, blocking collectives, send(): lax.all_to_all(space_field, 'dip', split_axis=1, concat_axis=2, tiled=True)  28.6 us
    dot_general x2, matrix products, receive(): space_rows = jnp.einsum('kx,kz->xz', moved, table, precision=precise)  22.1 us
    dot_general x2, matrix products, send(): jnp.einsum('kz,xz->kx', table, spread.reshape(3 * rows, dip_cells), preci...  17.4 us
    mul x3, other arithmetic, delay_term(): force_strike = (mix_along * spectrum[0] + mix_cross * spectrum[1]) * active  16.1 us
  transfers between devices with their start and end apart: 2, of which 1 were waited for; matrix products, arithmetic and copies ran while one was open for 29% of the time, Pallas kernels for 0%

profile of v1, /device:TPU:0, one launch (start us, length us, event | category | flops | bytes accessed | tf_op | source)
XLA Modules:
  0.0 610.2 jit_solution(13072024282742180843)
XLA Ops:
  0.6 3.8 copy.110
  4.5 4.5 all-to-all-start
  9.1 8.7 %multiply_add_fusion.5 = (f32[32,4096]{1,0:T(8,128)}, f32[32,4096]{1,0:T(8,128)}, f32[32,4096]{1,0:T(8,128)}, f32[32,4096]{1,0:T(8,128)}, f32[32,4096]{1,0:T(8,1...) fusion(f32[32]{0:T(128)S(1)} %get-tuple-element.69, ...), kind=kLoop, calls=%fused_computation.133 | loop fusion | flops 9568256 | bytes 6328608 | tf_op jit(solution)/shard_map/add | solution.py:418
  17.8 3.9 slice_convert_fusion
  21.7 13.6 %all-to-all-done = f32[3,512,256]{2,0,1:T(4,128)} async-done(((f32[3,512,256]{2,0,1:T(4,128)}), f32[3,512,256]{2,0,1:T(4,128)}, u32[]{:S(2)}, u32[]{:S(2)}) %all-to-all-start) | async-done | bytes 1572896 | tf_op jit(solution)/shard_map/all_to_all | solution.py:445
  35.3 3.7 copy.147
  42.0 10.7 %fusion.68 = f32[32,64,384]{2,1,0:T(8,128)} fusion(f32[32,64,1024]{2,1,0:T(8,128)} %constant.110, f32[384,1024,1]{1,0,2:T(8,128)} %reshape.1289), kind=kOutput, calls=%fused_computation.186 | convolution fusion | flops 4831838208 | bytes 13107200 | tf_op jit(solution)/shard_map/kz,xz->kx/dot_general | solution.py:446
  52.7 6.1 %all-to-all-start.1 = ((f32[32,64,384]{2,1,0:T(8,128)}), f32[32,64,384]{2,1,0:T(8,128)}, u32[]{:S(2)}, u32[]{:S(2)}) async-start(f32[32,64,384]{2,1,0:T(8,128)} %fusion.68), calls=%async_computation.1 | async-start | bytes 6291456 | tf_op jit(solution)/shard_map/all_to_all | solution.py:449
  61.0 5.6 add_multiply_fusion.7
  66.6 3.8 stack.108
  70.4 3.6 copy.123
  74.0 3.8 stack.109
  77.7 3.7 copy.124
  81.4 3.9 stack.110
  85.3 3.6 copy.125
  88.9 6.9 %add_multiply_fusion.5 = (f32[1,2,32,4096]{3,2,1,0:T(8,128)}, f32[1,2,32,4096]{3,2,1,0:T(8,128)}, f32[1,2,32,4096]{3,2,1,0:T(8,128)}, f32[1,2,32,4096]{3,2,1,0:T...) fusion(f32[1,3,2,32,4096]{4,3,2,1,0:T(8,128)} %get-tuple-element.11, f32[32,4096]{1,0:T(8,128)} %get-tuple-element.43, ...), kind=kLoop, calls=%fused_computation.31 | loop fusion | flops 5242880 | bytes 15204352 | tf_op jit(solution)/shard_map/mul | solution.py:61
  95.8 3.8 stack.112
  103.2 3.8 stack.113
  110.6 3.8 stack.114
  114.3 4.0 copy.128
  121.9 4.1 copy.129
  125.9 5.6 reshape.1285.refs_4_
  131.5 3.8 stack.99
  138.9 3.8 stack.100
  146.2 3.8 stack.101
  150.0 3.6 copy.117
  153.6 3.8 stack.103
  161.0 3.8 stack.104
  164.7 3.6 copy.119
  168.3 3.8 stack.105
  172.1 3.8 copy.120
  182.5 3.8 stack.95
  186.3 3.7 copy.112
  192.8 3.7 copy.113
  199.2 3.7 copy.114
  208.8 3.8 reshape.1284.refs_2_
  215.0 6.1 multiply_add_fusion.3
  224.5 7.5 %shard_map.122 = (f32[32,2,32,384]{3,2,1,0:T(8,128)S(1)}, f32[3,32,32,256]{3,2,1,0:T(8,128)S(1)}) custom-call(f32[32,2,32,384]{3,2,1,0:T(8,128)} %bitcast.3.refs_0_, f32[4,32,32,128]{3,2,1,0:T(8,128)S(1)} %pad_maximum_fusion.refs_1_, f32[3,32,32,256]{3,2,1,0:T(8,128)} %reshape.1284.refs_2_, f32[4,32,32,128]{3,2,1,0:T(8,128)S(1)} %copy-done, ...), custom_call_target="tpu_custom_call" | custom-call | flops 2415919104 | bytes 12582912 | tf_op jit(solution)/shard_map/pallas_call | solution.py:358
  232.0 77.4 %all_to_all.99 = f32[32,64,384]{2,1,0:T(8,128)} all-to-all(f32[32,64,384]{2,1,0:T(8,128)S(1)} %bitcast.220), channel_id=1, replica_groups=mesh['strike'=8,'dip'=4] {'strike','dip'}, dimensions={0} | all-to-all | bytes 6291456 | tf_op jit(solution)/shard_map/all_to_all | solution.py:455
  313.0 11.0 %fusion.69 = f32[3,128,1024]{2,1,0:T(8,128)} fusion(f32[3,128,2048]{2,1,0:T(8,128)} %bitcast.227, f32[2048,1024,1]{1,0,2:T(8,128)} %constant.111), kind=kOutput, calls=%fused_computation.187 | convolution fusion | flops 4831838208 | bytes 13107200 | tf_op jit(solution)/shard_map/kx,kz->xz/dot_general | solution.py:462
  326.9 30.1 %all_to_all.100 = f32[3,128,1024]{1,0,2:T(4,128)} all-to-all(f32[3,128,1024]{1,0,2:T(4,128)} %copy.131), channel_id=1, replica_groups=mesh['strike'=8,'dip'=4] {'dip'}, dimensions={2} | all-to-all | bytes 3145728 | tf_op jit(solution)/shard_map/all_to_all | solution.py:463
  367.4 28.6 %all_to_all.101 = f32[3,512,256]{2,0,1:T(4,128)S(1)} all-to-all(f32[3,512,256]{2,0,1:T(4,128)S(1)} %pad_maximum_fusion.1), channel_id=1, replica_groups=mesh['strike'=8,'dip'=4] {'dip'}, dimensions={1} | all-to-all | bytes 3145728 | tf_op jit(solution)/shard_map/all_to_all | solution.py:445
  397.4 6.7 %fusion.70 = f32[2048,384]{1,0:T(8,128)S(1)} fusion(f32[2048,1024]{1,0:T(8,128)S(1)} %bitcast.222, f32[384,1024]{1,0:T(8,128)S(1)} %bitcast.234), kind=kOutput, calls=%fused_computation.188 | convolution fusion | flops 4831838208 | bytes 13107200 | tf_op jit(solution)/shard_map/kz,xz->kx/dot_general | solution.py:446
  404.1 73.8 %all_to_all.102 = f32[32,64,384]{2,1,0:T(8,128)S(1)} all-to-all(f32[32,64,384]{2,1,0:T(8,128)S(1)} %bitcast.223), channel_id=1, replica_groups=mesh['strike'=8,'dip'=4] {'strike','dip'}, dimensions={0} | all-to-all | bytes 6291456 | tf_op jit(solution)/shard_map/all_to_all | solution.py:449
  477.9 5.5 shard_map.123
  483.4 74.9 %all_to_all.103 = f32[32,64,384]{2,1,0:T(8,128)S(1)} all-to-all(f32[32,64,384]{2,1,0:T(8,128)S(1)} %bitcast.219), channel_id=1, replica_groups=mesh['strike'=8,'dip'=4] {'strike','dip'}, dimensions={0} | all-to-all | bytes 6291456 | tf_op jit(solution)/shard_map/all_to_all | solution.py:455
  560.6 11.0 %fusion.71 = f32[3,128,1024]{2,1,0:T(8,128)} fusion(f32[3,128,2048]{2,1,0:T(8,128)} %bitcast.226, f32[2048,1024,1]{1,0,2:T(8,128)} %constant.111), kind=kOutput, calls=%fused_computation.189 | convolution fusion | flops 4831838208 | bytes 13107200 | tf_op jit(solution)/shard_map/kx,kz->xz/dot_general | solution.py:462
  573.6 28.9 %all_to_all.104 = f32[3,128,1024]{1,0,2:T(4,128)} all-to-all(f32[3,128,1024]{1,0,2:T(4,128)S(1)} %copy.138), channel_id=1, replica_groups=mesh['strike'=8,'dip'=4] {'dip'}, dimensions={2} | all-to-all | bytes 3145728 | tf_op jit(solution)/shard_map/all_to_all | solution.py:463
  (91 shorter events, 80.1 us)
Async XLA Ops:
  4.5 30.8 %all-to-all-start = ((f32[3,512,256]{2,0,1:T(4,128)}), f32[3,512,256]{2,0,1:T(4,128)}, u32[]{:S(2)}, u32[]{:S(2)}) async-start(f32[3,512,256]{2,0,1:T(4,128)} %copy.110), calls=%async_computation | async-start | bytes 4194304 | tf_op jit(solution)/shard_map/all_to_all | solution.py:445
  9.0 8.7 %copy-start.15 = (bf16[4,3,2,32,4096]{4,3,2,1,0:T(8,128)(2,1)S(1)}, bf16[4,3,2,32,4096]{4,3,2,1,0:T(8,128)(2,1)}, u32[]{:S(2)}) copy-start(bf16[4,3,2,32,4096]{4,3,2,1,0:T(8,128)(2,1)} %param.12) | copy-start | bytes 18874372
  52.7 170.2 %all-to-all-start.1 = ((f32[32,64,384]{2,1,0:T(8,128)}), f32[32,64,384]{2,1,0:T(8,128)}, u32[]{:S(2)}, u32[]{:S(2)}) async-start(f32[32,64,384]{2,1,0:T(8,128)} %fusion.68), calls=%async_computation.1 | async-start | bytes 6291456 | tf_op jit(solution)/shard_map/all_to_all | solution.py:449
  186.3 3.7 copy-start.14
  192.8 3.7 copy-start.13
  199.2 3.8 copy-start.10
  199.2 3.8 copy-start.11
  199.2 3.8 copy-start.12
  221.2 1.6 copy-start.3
  221.3 1.6 copy-start.4
  221.3 1.6 copy-start.5
  222.9 1.6 copy-start
  232.0 77.4 %copy-start.1 = (f32[3,32,32,256]{3,2,1,0:T(8,128)}, f32[3,32,32,256]{3,2,1,0:T(8,128)S(1)}, u32[]{:S(2)}) copy-start(f32[3,32,32,256]{3,2,1,0:T(8,128)S(1)} %get-tuple-element.5.refs_2_) | copy-start | bytes 9437188
  357.0 4.4 copy-start.16
  359.8 1.7 copy-start.6
  359.8 1.8 copy-start.19
  359.8 2.0 copy-start.20
  364.3 1.2 copy-start.8
  365.5 31.9 %slice-start = ((s8[8388608]{0:T(1024)(128)(4,1)}), s8[4194304]{0:T(1024)(128)(4,1)S(1)}, s32[]{:S(2)}) async-start(s8[8388608]{0:T(1024)(128)(4,1)} %bitcast.221), calls=%async_computation.8 | async-start | bytes 8388608
  367.4 30.0 %slice-start.1 = ((s8[8388608]{0:T(1024)(128)(4,1)}), s8[4194304]{0:T(1024)(128)(4,1)S(1)}, s32[]{:S(2)}) async-start(s8[8388608]{0:T(1024)(128)(4,1)} %bitcast.221), calls=%async_computation.9 | async-start | bytes 8388608
  404.1 73.8 %copy-start.2 = (f32[3,32,32,256]{3,2,1,0:T(8,128)S(1)}, f32[3,32,32,256]{3,2,1,0:T(8,128)}, u32[]{:S(2)}) copy-start(f32[3,32,32,256]{3,2,1,0:T(8,128)} %copy-done.1) | copy-start | bytes 9437188
  602.6 2.1 copy-start.7
  602.6 2.1 copy-start.9
  604.5 1.1 copy-start.17
  604.5 1.2 copy-start.18

commit v2 on v1

--- a/solution.py
+++ b/solution.py
@@ -64,11 +64,10 @@
     return jnp.stack([force_strike, force_dip, force_open])
 
 
-def friction_step(force_field, prestress, normal_stress, direct_effect, state_log):
+def friction_planes(force_field, prestress, strength, state_log):
     load_strike = prestress[0] + force_field[0]
     load_dip = prestress[1] + force_field[1]
     traction = jnp.sqrt(load_strike * load_strike + load_dip * load_dip)
-    strength = direct_effect * normal_stress
     factor = 2.0 * radiation * jnp.exp(-state_log)
     estimate = jnp.minimum(traction / strength, area_sine(traction / factor))
     for repeat in range(NEWTON):
@@ -76,11 +75,16 @@
         estimate = estimate + residual / (strength + factor * jnp.cosh(estimate))
     slip_speed = (traction - strength * estimate) / radiation
     unit_scale = slip_speed / jnp.maximum(traction, 1.0)
-    new_rates = jnp.stack(
-        [unit_scale * load_strike, unit_scale * load_dip, force_field[2] / radiation]
-    )
+    new_rates = [unit_scale * load_strike, unit_scale * load_dip, force_field[2] / radiation]
     new_state = state_log + time_step * (healing * jnp.exp(-state_log) - slip_speed / slip_length)
     return (new_rates, new_state)
+
+
+def friction_step(force_field, prestress, normal_stress, direct_effect, state_log):
+    new_rates, new_state = friction_planes(
+        force_field, prestress, direct_effect * normal_stress, state_log
+    )
+    return (jnp.stack(new_rates), new_state)
 
 
 def phase_table(first_index, second_index, period):
@@ -305,19 +309,19 @@
         spec[comp] = split_product(
             line[comp].reshape(rows, width), high_ref[0], low_ref[0]
         ).reshape(blocks, SUBLANES, width)
-    for half in halves:
+    for part, half in enumerate(halves):
         along, across, opening = (spec[comp, :, :, half] for comp in range(3))
-        line[0, :, :, half] = mix_ref[0] * along + mix_ref[1] * across + add_ref[0, :, :, half]
-        line[1, :, :, half] = mix_ref[1] * along + mix_ref[2] * across + add_ref[1, :, :, half]
-        line[2, :, :, half] = mix_ref[3] * opening + add_ref[2, :, :, half]
+        line[0, :, :, half] = mix_ref[0] * along + mix_ref[1] * across + add_ref[0, part]
+        line[1, :, :, half] = mix_ref[1] * along + mix_ref[2] * across + add_ref[1, part]
+        line[2, :, :, half] = mix_ref[3] * opening + add_ref[2, part]
         if keep:
-            later_out_ref[0, :, :, half] = (
-                later_mix_ref[0] * along + later_mix_ref[1] * across + later_ref[0, :, :, half]
+            later_out_ref[0, part] = (
+                later_mix_ref[0] * along + later_mix_ref[1] * across + later_ref[0, part]
             )
-            later_out_ref[1, :, :, half] = (
-                later_mix_ref[1] * along + later_mix_ref[2] * across + later_ref[1, :, :, half]
+            later_out_ref[1, part] = (
+                later_mix_ref[1] * along + later_mix_ref[2] * across + later_ref[1, part]
             )
-            later_out_ref[2, :, :, half] = later_mix_ref[3] * opening + later_ref[2, :, :, half]
+            later_out_ref[2, part] = later_mix_ref[3] * opening + later_ref[2, part]
     for comp in range(3):
         own = slice(comp * LANES, (comp + 1) * LANES)
         spec[comp] = split_product(
@@ -342,7 +346,7 @@
     tiles = modes // SUBLANES
     wide = pl.BlockSpec((blocks, 2, SUBLANES, depth), lambda tile: (0, 0, tile, 0))
     factors = pl.BlockSpec((4, blocks, SUBLANES, LANES), lambda tile: (0, 0, tile, 0))
-    field = pl.BlockSpec((3, blocks, SUBLANES, 2 * LANES), lambda tile: (0, 0, tile, 0))
+    field = pl.BlockSpec((3, 2, blocks, SUBLANES, LANES), lambda tile: (0, 0, 0, tile, 0))
     fixed = [
         pl.BlockSpec(item.shape, lambda tile, rank=item.ndim: (0,) * rank) for item in tables
     ]
@@ -391,12 +395,13 @@
     return jnp.asarray(bend, jnp.float32), jnp.asarray(high), jnp.asarray(low)
 
 
-def dip_table(devices, dip_cells):
+def dip_tables(devices, dip_cells):
     modes = np.arange(dip_cells)
     angle = 2.0 * np.pi * (modes[:, None] * modes[None, :] % dip_cells) / dip_cells
     pair = np.stack([np.cos(angle), -np.sin(angle)]) / math.sqrt(dip_cells)
     pair = pair.reshape(2, devices, dip_cells // devices, dip_cells).transpose(1, 0, 2, 3)
-    return jnp.asarray(pair.reshape(2 * dip_cells, dip_cells), jnp.float32)
+    pair = pair.reshape(2 * dip_cells, dip_cells)
+    return jnp.asarray(pair, jnp.float32), jnp.asarray(pair.T, jnp.float32)
 
 
 def all_mixing(geometry):
@@ -435,17 +440,28 @@
     strike_cells = history.shape[4]
     rows = row_count // dip_count
     own = lax.axis_index("strike") * dip_count + lax.axis_index("dip")
-    table = dip_table(devices, dip_cells)
+    table, back_table = dip_tables(devices, dip_cells)
     tables = strike_tables(devices, strike_cells)
     local_modes = own * modes + jnp.arange(modes, dtype=jnp.int32)
     strike_modes = jnp.arange(strike_cells, dtype=jnp.int32)
     precise = lax.Precision.HIGH
 
-    def send(space_field):
-        spread = lax.all_to_all(space_field, "dip", split_axis=1, concat_axis=2, tiled=True)
-        dip_spec = jnp.einsum(
-            "kz,xz->kx", table, spread.reshape(3 * rows, dip_cells), precision=precise
-        )
+    def to_rows(planes):
+        count = planes.shape[0]
+        parts = planes.reshape(count, dip_count, rows, -1)
+        parts = jnp.transpose(parts, (1, 3, 0, 2)).reshape(dip_count, -1, count * rows)
+        moved = lax.all_to_all(parts, "dip", split_axis=0, concat_axis=0, tiled=True)
+        return moved.reshape(dip_cells, count * rows)
+
+    def from_rows(space_rows):
+        count = space_rows.shape[1] // rows
+        parts = space_rows.reshape(dip_count, -1, count * rows)
+        moved = lax.all_to_all(parts, "dip", split_axis=0, concat_axis=0, tiled=True)
+        moved = moved.reshape(dip_count, -1, count, rows)
+        return jnp.transpose(moved, (2, 0, 3, 1)).reshape(count, row_count, -1)
+
+    def send(space_rows):
+        dip_spec = jnp.dot(table, space_rows, precision=precise)
         moved = lax.all_to_all(
             dip_spec, ("strike", "dip"), split_axis=0, concat_axis=0, tiled=True
         )
@@ -459,10 +475,12 @@
             concat_axis=0,
             tiled=True,
         )
-        space_rows = jnp.einsum("kx,kz->xz", moved, table, precision=precise)
-        return lax.all_to_all(
-            space_rows.reshape(3, rows, dip_cells), "dip", split_axis=2, concat_axis=1, tiled=True
-        )
+        return planes_of(jnp.dot(back_table, moved, precision=precise))
+
+    def planes_of(space_rows):
+        return [
+            space_rows[:, start : start + rows] for start in range(0, space_rows.shape[1], rows)
+        ]
 
     def by_residue(plain):
         lead = plain.shape[:-1]
@@ -481,25 +499,30 @@
     )
 
     def past(first):
-        summed = 0.0
+        strike_sum, dip_sum, open_sum = 0.0, 0.0, 0.0
         for offset in range(first, HIST):
+            along, cross, across, opening = plain_mixing[offset]
             active = (offset < lengths).astype(jnp.float32)
             source = history[offset - first].astype(jnp.float32)
-            summed = summed + delay_term(source, plain_mixing[offset], active)
-        summed = jnp.transpose(by_residue(summed), (0, 4, 2, 1, 3))
-        return summed.reshape(3, devices, modes, 2 * rows)
-
-    arrived = send(slip_rate)
+            strike_sum += (along * source[0] + cross * source[1]) * active
+            dip_sum += (cross * source[0] + across * source[1]) * active
+            open_sum += opening * source[2] * active
+        summed = jnp.stack([strike_sum, dip_sum, open_sum])
+        return jnp.transpose(by_residue(summed), (0, 1, 4, 2, 3))
+
+    arrived = send(to_rows(slip_rate))
+    load = jnp.concatenate(
+        [prestress, (direct_effect * normal_stress)[None], state_log[None]]
+    )
+    load_strike, load_dip, strength, state = planes_of(to_rows(load))
     strike_rows, addend = strike_pass(
         arrived, mixing, past(1), tables, (later_mixing, past(2))
     )
-    next_rates, next_state = friction_step(
-        receive(strike_rows), prestress, normal_stress, direct_effect, state_log
-    )
-    (strike_rows,) = strike_pass(send(next_rates), mixing, addend, tables)
-    return friction_step(
-        receive(strike_rows), prestress, normal_stress, direct_effect, next_state
-    )
+    rates, state = friction_planes(receive(strike_rows), (load_strike, load_dip), strength, state)
+    (strike_rows,) = strike_pass(send(jnp.concatenate(rates, axis=1)), mixing, addend, tables)
+    rates, state = friction_planes(receive(strike_rows), (load_strike, load_dip), strength, state)
+    result = from_rows(jnp.concatenate(rates + [state], axis=1))
+    return (result[:3], result[3])
 
 
 def choose(slip_rate, history, *others):

time: 619 us -> 452 us (0.73)
  blocking collectives: 314 us -> 178 us
  local copies, waits for them, and re-layouts: 163 us -> 69.6 us
  waiting for transfers between devices: 13.6 us -> 85 us
  starting transfers between devices: 10.6 us -> 21.2 us
  other arithmetic: 55.9 us -> 47.5 us
  matrix products: 39.5 us -> 31.3 us
    all_to_all x2 -> x1, blocking collectives: 152 us -> 74.9 us  [receive(): lax.all_to_all(strike_rows.reshape(2 * dip_cells, 3 * rows), ('strike', '...]
    all_to_all x1 -> x3, waiting for transfers between devices: 13.6 us -> 85 us  [the longest x1 68.2 us: receive(): lax.all_to_all(strike_rows.reshape(2 * dip_cells, 3 * rows), ('strike', '...]
    another operation x32 -> x12, local copies, waits for them, and re-layouts: 111 us -> 45.6 us  [past(): summed = jnp.stack([strike_sum, dip_sum, open_sum])]
    all_to_all x3 -> x1, blocking collectives: 87.7 us -> 28.3 us  [from_rows(): lax.all_to_all(parts, 'dip', split_axis=0, concat_axis=0, tiled=True)]
    all_to_all x6 -> x1, local copies, waits for them, and re-layouts: 15.4 us -> 1.61 us  [to_rows(): lax.all_to_all(parts, 'dip', split_axis=0, concat_axis=0, tiled=True)]
    add x1 -> x3, other arithmetic: 2.65 us -> 14.4 us  [the longest x1 6.68 us: past(): dip_sum += (cross * source[0] + across * source[1]) * active]
    all_to_all x1 -> x3, starting transfers between devices: 4.49 us -> 15.4 us  [the longest x2 8.68 us: to_rows(): lax.all_to_all(parts, 'dip', split_axis=0, concat_axis=0, tiled=True)]
    mul x4 -> x5, other arithmetic: 16.4 us -> 5.93 us  [the longest x2 3.75 us: friction_planes(): unit_scale * load_strike]
  transfers between devices with their start and end apart: 2 -> 4, of which waited for: 1 -> 2; matrix products, arithmetic and copies ran while one was open for 29% -> 22% of each run, Pallas kernels for 0% -> 2%
where the time goes in v2:
time: 452 us; the launch traced here: 447 us
  blocking collectives  178 us (39%)
  waiting for transfers between devices  85 us (19%)
  local copies, waits for them, and re-layouts  69.6 us (15%)
  other arithmetic  47.5 us (11%)
  matrix products  31.3 us (7%)
  starting transfers between devices  21.2 us (5%)
  Pallas kernels  13.1 us (3%)
    all_to_all x1, blocking collectives, send(): lax.all_to_all(dip_spec, ('strike', 'dip'), split_axis=0, concat_axis=0,...  74.9 us
    all_to_all x1, blocking collectives, receive(): lax.all_to_all(strike_rows.reshape(2 * dip_cells, 3 * rows), ('strike', '...  74.9 us
    all_to_all x1, waiting for transfers between devices, receive(): lax.all_to_all(strike_rows.reshape(2 * dip_cells, 3 * rows), ('strike', '...  68.2 us
    another operation x12, local copies, waits for them, and re-layouts, past(): summed = jnp.stack([strike_sum, dip_sum, open_sum])  45.6 us
    all_to_all x1, blocking collectives, from_rows(): lax.all_to_all(parts, 'dip', split_axis=0, concat_axis=0, tiled=True)  28.3 us
    dot_general x2, matrix products, send(): dip_spec = jnp.dot(table, space_rows, precision=precise)  17.5 us
    all_to_all x2, waiting for transfers between devices, to_rows(): lax.all_to_all(parts, 'dip', split_axis=0, concat_axis=0, tiled=True)  16.8 us
    add x2, other arithmetic, all_mixing(): square_strike * two + square_dip * three  14.1 us
  transfers between devices with their start and end apart: 4, of which 2 were waited for; matrix products, arithmetic and copies ran while one was open for 22% of the time, Pallas kernels for 2%

profile of v2, /device:TPU:0, one launch (start us, length us, event | category | flops | bytes accessed | tf_op | source)
XLA Modules:
  0.0 447.1 jit_solution(9118623480203558409)
XLA Ops:
  0.6 2.7 copy.43
  3.3 4.2 all-to-all-start.1
  8.8 2.0 reshape.1259
  10.9 16.8 %all-to-all-done.1 = f32[4,256,384]{1,2,0:T(8,128)S(1)} async-done(((f32[4,256,384]{1,2,0:T(8,128)}), f32[4,256,384]{1,2,0:T(8,128)S(1)}, u32[]{:S(2)}, u32[]{:S(2)}) %all-to-all-start.1) | async-done | bytes 1572896 | tf_op jit(solution)/shard_map/all_to_all | solution.py:453
  27.6 1.6 copy.44
  29.3 10.7 %fusion.74 = f32[32,64,384]{2,1,0:T(8,128)} fusion(f32[32,64,1024]{2,1,0:T(8,128)} %constant.113, f32[1024,384,1]{1,0,2:T(8,128)} %bitcast.152), kind=kOutput, calls=%fused_computation.180 | convolution fusion | flops 4831838208 | bytes 13107200 | tf_op jit(solution)/shard_map/dot_general | solution.py:464
  40.0 5.9 %all-to-all-start.2 = ((f32[32,64,384]{2,1,0:T(8,128)}), f32[32,64,384]{2,1,0:T(8,128)S(1)}, u32[]{:S(2)}, u32[]{:S(2)}) async-start(f32[32,64,384]{2,1,0:T(8,128)} %fusion.74), calls=%async_computation.2 | async-start | bytes 6291456 | tf_op jit(solution)/shard_map/all_to_all | solution.py:465
  45.8 8.0 %multiply_add_fusion.14 = (f32[32,4096]{1,0:T(8,128)S(1)}, f32[32,4096]{1,0:T(8,128)}, f32[32,4096]{1,0:T(8,128)S(1)}, f32[32,4096]{1,0:T(8,128)}, f32[32,4096]{...) fusion(f32[32]{0:T(128)S(1)} %get-tuple-element.50, ...), kind=kLoop, calls=%fused_computation.132 | loop fusion | flops 9568256 | bytes 6328608 | tf_op jit(solution)/shard_map/add | solution.py:423
  53.9 4.2 slice_convert_fusion.1
  58.2 3.0 multiply_add_fusion.2
  62.4 3.8 stack.44
  66.2 3.7 copy.49
  69.9 6.7 %multiply_add_fusion.1 = (f32[1,2,32,4096]{3,2,1,0:T(8,128)}, f32[1,2,32,4096]{3,2,1,0:T(8,128)}) fusion(f32[1,3,2,32,4096]{4,3,2,1,0:T(8,128)} %copy-done.10, f32[1,3,2,32,4096]{4,3,2,1,0:T(8,128)} %copy-done.9, f32[32,4096]{1,0:T(8,128)} %get-tuple-element.36, f32[32,4096]{1,0:T(8,128)} %get-tuple-element.34, f32[32,4096]{1,0:T(8,128)} %get-tuple-element.25, ...), kind=kLoop, calls=%fused_computation.29 | loop fusion | flops 6029312 | bytes 13107200 | tf_op jit(solution)/shard_map/add | solution.py:508
  76.5 3.8 stack.45
  80.3 3.7 copy.50
  84.1 4.7 %multiply_add_fusion = (f32[1,2,32,4096]{3,2,1,0:T(8,128)}, f32[1,2,32,4096]{3,2,1,0:T(8,128)}) fusion(f32[1,3,2,32,4096]{4,3,2,1,0:T(8,128)} %copy-done.10, f32[1,3,2,32,4096]{4,3,2,1,0:T(8,128)} %copy-done.9, f32[32,4096]{1,0:T(8,128)} %get-tuple-element.44, f32[32,4096]{1,0:T(8,128)} %get-tuple-element.45, f32[32,4096]{1,0:T(8,128)} %get-tuple-element.25, ...), kind=kLoop, calls=%fused_computation.28 | loop fusion | flops 3407872 | bytes 8388608 | tf_op jit(solution)/shard_map/add | solution.py:509
  88.8 3.8 stack.46
  92.6 3.8 copy.51
  96.4 3.8 stack.39
  100.2 3.7 copy.45
  103.9 3.8 stack.40
  107.7 3.7 copy.46
  111.4 4.2 stack.41
  115.6 3.7 copy.47
  119.3 3.0 copy.48
  122.3 1.3 mul.1943
  123.6 2.9 pad_maximum_fusion
  126.6 4.5 all-to-all-start
  131.1 6.1 %multiply_add_fusion.8 = (f32[1,32,32,128]{3,2,1,0:T(8,128)S(1)}, f32[1,32,32,128]{3,2,1,0:T(8,128)S(1)}, f32[1,32,32,128]{3,2,1,0:T(8,128)S(1)}, f32[1,32,32,12...) fusion(f32[32]{0:T(128)S(1)} %get-tuple-element.50, ...), kind=kLoop, calls=%fused_computation.122 | loop fusion | flops 6291456 | bytes 4231456 | tf_op jit(solution)/shard_map/add | solution.py:423
  139.0 2.0 maximum_bitcast_fusion.1.refs_4_
  142.0 2.1 maximum_bitcast_fusion.refs_2_
  144.4 1.6 copy-done.1
  146.1 7.4 %shard_map.131 = (f32[32,2,32,384]{3,2,1,0:T(8,128)S(1)}, f32[3,2,32,32,128]{4,3,2,1,0:T(8,128)S(1)}) custom-call(f32[32,2,32,384]{3,2,1,0:T(8,128)S(1)} %bitcast.131, f32[4,32,32,128]{3,2,1,0:T(8,128)S(1)} %pad_maximum_fusion.1.refs_1_, f32[3,2,32,32,128]{4,3,2,1,0:T(8,128)} %maximum_bitcast_fusion.refs_2_, ...), custom_call_target="tpu_custom_call" | custom-call | flops 2415919104 | bytes 12582912 | tf_op jit(solution)/shard_map/pallas_call | solution.py:362
  153.5 1.7 copy-done.2
  155.2 1.6 copy-done.3
  156.8 6.7 %all-to-all-start.3 = ((f32[32,64,384]{2,1,0:T(8,128)}), f32[32,64,384]{2,1,0:T(8,128)}, u32[]{:S(2)}, u32[]{:S(2)}) async-start(f32[32,64,384]{2,1,0:T(8,128)} %bitcast.134), calls=%async_computation.3 | async-start | bytes 6291456 | tf_op jit(solution)/shard_map/all_to_all | solution.py:471
  163.5 3.3 copy.55
  166.8 68.2 %all-to-all-done.3 = f32[32,64,384]{2,1,0:T(8,128)} async-done(((f32[32,64,384]{2,1,0:T(8,128)}), f32[32,64,384]{2,1,0:T(8,128)}, u32[]{:S(2)}, u32[]{:S(2)}) %all-to-all-start.3) | async-done | bytes 3145760 | tf_op jit(solution)/shard_map/all_to_all | solution.py:471
  235.0 8.8 %fusion.75 = f32[1024,384]{0,1:T(8,128)S(1)} fusion(f32[1024,2048]{1,0:T(8,128)} %constant.109.clone, f32[2048,384]{1,0:T(8,128)} %bitcast.26), kind=kOutput, calls=%fused_computation.181 | convolution fusion | flops 4831838208 | bytes 13107200 | tf_op jit(solution)/shard_map/dot_general | solution.py:478
  243.8 1.8 fusion.60
  246.0 6.8 %fusion = f32[2048,384]{1,0:T(8,128)S(1)} fusion(f32[2048,1024]{1,0:T(8,128)S(1)} %bitcast.143, f32[1024,128]{0,1:T(8,128)S(1)} %get-tuple-element.23, f32[1024,128]{0,1:T(8,128)S(1)} %get-tuple-element.22, f32[1024,128]{0,1:T(8,128)S(1)} %get-tuple-element.8), kind=kOutput, calls=%fused_computation.7 | convolution fusion | flops 4832624640 | bytes 13107200 | tf_op jit(solution)/shard_map/dot_general | solution.py:464
  252.8 74.9 %all_to_all.54 = f32[32,64,384]{2,1,0:T(8,128)S(1)} all-to-all(f32[32,64,384]{2,1,0:T(8,128)S(1)} %bitcast.141), channel_id=1, replica_groups=mesh['strike'=8,'dip'=4] {'strike','dip'}, dimensions={0} | all-to-all | bytes 6291456 | tf_op jit(solution)/shard_map/all_to_all | solution.py:465
  327.7 5.6 %shard_map.132 = f32[32,2,32,384]{3,2,1,0:T(8,128)S(1)} custom-call(f32[32,2,32,384]{3,2,1,0:T(8,128)S(1)} %bitcast.132, f32[4,32,32,128]{3,2,1,0:T(8,128)S(1)} %pad_maximum_fusion.1.refs_1_, f32[3,2,32,32,128]{4,3,2,1,0:T(8,128)S(1)} %copy-done.4, f32[2,32,128]{2,1,0:T(8,128)S(1)} %copy-done.7, bf16[2,256,256]{2,1,0:T(8,128)(2,1)S(1)} %copy-done.5, ...), custom_call_target="tpu_custom_call" | custom-call | flops 2415919104 | bytes 12582912 | tf_op jit(solution)/shard_map/pallas_call | solution.py:362
  333.4 74.9 %all_to_all.55 = f32[32,64,384]{2,1,0:T(8,128)S(1)} all-to-all(f32[32,64,384]{2,1,0:T(8,128)S(1)} %bitcast.133), channel_id=1, replica_groups=mesh['strike'=8,'dip'=4] {'strike','dip'}, dimensions={0} | all-to-all | bytes 6291456 | tf_op jit(solution)/shard_map/all_to_all | solution.py:471
  408.3 5.1 %fusion.76 = f32[1024,384]{0,1:T(8,128)S(1)} fusion(f32[1024,2048]{1,0:T(8,128)S(1)} %bitcast.136, f32[2048,384]{1,0:T(8,128)S(1)} %bitcast.144), kind=kOutput, calls=%fused_computation.182 | convolution fusion | flops 4831838208 | bytes 13107200 | tf_op jit(solution)/shard_map/dot_general | solution.py:478
  413.3 1.9 fusion.62
  416.2 28.3 %all_to_all.56 = f32[4,256,512]{1,2,0:T(8,128)S(1)} all-to-all(f32[4,256,512]{1,2,0:T(8,128)S(1)} %bitcast.150), channel_id=1, replica_groups=mesh['strike'=8,'dip'=4] {'dip'}, dimensions={0} | all-to-all | bytes 4194304 | tf_op jit(solution)/shard_map/all_to_all | solution.py:459
  445.6 1.3 copy.53
  (79 shorter events, 8.1 us)
Async XLA Ops:
  0.6 6.9 %copy-start.26 = (s32[32,4096]{1,0:T(8,128)S(1)}, s32[32,4096]{1,0:T(8,128)}, u32[]{:S(2)}) copy-start(s32[32,4096]{1,0:T(8,128)} %param.14) | copy-start | bytes 1572868
  3.3 24.3 %all-to-all-start.1 = ((f32[4,256,384]{1,2,0:T(8,128)}), f32[4,256,384]{1,2,0:T(8,128)S(1)}, u32[]{:S(2)}, u32[]{:S(2)}) async-start(f32[4,256,384]{1,2,0:T(8,128)} %bitcast.151), calls=%async_computation.1 | async-start | bytes 3145728 | tf_op jit(solution)/shard_map/all_to_all | solution.py:453
  8.8 31.2 %copy-start.12 = (f32[32,4096]{1,0:T(8,128)}, f32[32,4096]{1,0:T(8,128)S(1)}, u32[]{:S(2)}) copy-start(f32[32,4096]{1,0:T(8,128)S(1)} %get-tuple-element.24) | copy-start | bytes 1572868
  40.0 86.6 %all-to-all-start.2 = ((f32[32,64,384]{2,1,0:T(8,128)}), f32[32,64,384]{2,1,0:T(8,128)S(1)}, u32[]{:S(2)}, u32[]{:S(2)}) async-start(f32[32,64,384]{2,1,0:T(8,128)} %fusion.74), calls=%async_computation.2 | async-start | bytes 6291456 | tf_op jit(solution)/shard_map/all_to_all | solution.py:465
  53.9 4.3 copy-start.16
  53.9 4.3 copy-start.17
  53.9 4.3 copy-start.18
  53.9 4.3 copy-start.13
  53.9 4.3 copy-start.14
  53.9 4.3 copy-start.15
  58.1 3.1 copy-start.9
  58.1 3.3 copy-start.10
  58.1 4.2 copy-start.11
  126.6 10.6 %copy-start = (f32[32,64,384]{2,1,0:T(8,128)}, f32[32,64,384]{2,1,0:T(8,128)S(1)}, u32[]{:S(2)}) copy-start(f32[32,64,384]{2,1,0:T(8,128)S(1)} %all-to-all-done.2) | copy-start | bytes 9437188
  126.6 30.2 %all-to-all-start = ((f32[4,256,512]{1,2,0:T(8,128)}), f32[4,256,512]{1,2,0:T(8,128)}, u32[]{:S(2)}, u32[]{:S(2)}) async-start(f32[4,256,512]{1,2,0:T(8,128)} %bitcast.146), calls=%async_computation | async-start | bytes 4194304 | tf_op jit(solution)/shard_map/all_to_all | solution.py:453
  137.1 1.2 copy-start.19
  137.2 1.5 copy-start.20
  137.2 1.8 copy-start.21
  139.0 2.0 copy-start.22
  139.0 2.3 copy-start.23
  139.0 3.0 copy-start.24
  142.0 2.1 copy-start.25
  144.1 1.9 copy-start.1
  144.1 1.9 copy-start.5
  144.1 2.0 copy-start.6
  144.1 2.0 copy-start.7
  153.5 1.7 copy-start.2
  155.2 1.6 copy-start.3
  156.8 78.1 %all-to-all-start.3 = ((f32[32,64,384]{2,1,0:T(8,128)}), f32[32,64,384]{2,1,0:T(8,128)}, u32[]{:S(2)}, u32[]{:S(2)}) async-start(f32[32,64,384]{2,1,0:T(8,128)} %bitcast.134), calls=%async_computation.3 | async-start | bytes 6291456 | tf_op jit(solution)/shard_map/all_to_all | solution.py:471
  235.0 11.0 %slice-start.2 = ((s8[8388608]{0:T(1024)(128)(4,1)}), s8[4194304]{0:T(1024)(128)(4,1)S(1)}, s32[]{:S(2)}) async-start(s8[8388608]{0:T(1024)(128)(4,1)} %bitcast.142), calls=%async_computation.9 | async-start | bytes 8388608
  235.0 8.8 %copy-start.8 = (f32[4,64,8,256]{3,2,0,1:T(8,128)S(1)}, f32[4,64,8,256]{3,2,0,1:T(8,128)}, u32[]{:S(2)}) copy-start(f32[4,64,8,256]{3,2,0,1:T(8,128)} %copy.55) | copy-start | bytes 6291460
  235.0 11.0 %slice-start.3 = ((s8[8388608]{0:T(1024)(128)(4,1)}), s8[4194304]{0:T(1024)(128)(4,1)S(1)}, s32[]{:S(2)}) async-start(s8[8388608]{0:T(1024)(128)(4,1)} %bitcast.142), calls=%async_computation.10 | async-start | bytes 8388608
  252.8 75.0 %copy-start.4 = (f32[3,2,32,32,128]{4,3,2,1,0:T(8,128)S(1)}, f32[3,2,32,32,128]{4,3,2,1,0:T(8,128)}, u32[]{:S(2)}) copy-start(f32[3,2,32,32,128]{4,3,2,1,0:T(8,128)} %copy-done.3) | copy-start | bytes 9437188
  252.8 155.5 %slice-start = ((s8[8388608]{0:T(1024)(128)(4,1)}), s8[4194304]{0:T(1024)(128)(4,1)S(1)}, s32[]{:S(2)}) async-start(s8[8388608]{0:T(1024)(128)(4,1)} %bitcast.135), calls=%async_computation.7 | async-start | bytes 8388608
  327.7 80.5 %slice-start.1 = ((s8[8388608]{0:T(1024)(128)(4,1)}), s8[4194304]{0:T(1024)(128)(4,1)S(1)}, s32[]{:S(2)}) async-start(s8[8388608]{0:T(1024)(128)(4,1)} %bitcast.135), calls=%async_computation.8 | async-start | bytes 8388608

commit v3 on v2

--- a/solution.py
+++ b/solution.py
@@ -75,7 +75,7 @@
         estimate = estimate + residual / (strength + factor * jnp.cosh(estimate))
     slip_speed = (traction - strength * estimate) / radiation
     unit_scale = slip_speed / jnp.maximum(traction, 1.0)
-    new_rates = [unit_scale * load_strike, unit_scale * load_dip, force_field[2] / radiation]
+    new_rates = [unit_scale * load_strike, unit_scale * load_dip]
     new_state = state_log + time_step * (healing * jnp.exp(-state_log) - slip_speed / slip_length)
     return (new_rates, new_state)
 
@@ -84,7 +84,7 @@
     new_rates, new_state = friction_planes(
         force_field, prestress, direct_effect * normal_stress, state_log
     )
-    return (jnp.stack(new_rates), new_state)
+    return (jnp.stack(new_rates + [force_field[2] / radiation]), new_state)
 
 
 def phase_table(first_index, second_index, period):
@@ -283,18 +283,19 @@
     return dot(left_high, high) + (dot(left_low, high) + dot(left_high, low))
 
 
-def owner_kernel(keep, *refs):
-    if keep:
-        x_ref, mix_ref, add_ref, later_mix_ref, later_ref, bend_ref, high_ref, low_ref = refs[:8]
-        out_ref, later_out_ref, line, spec = refs[8:]
-    else:
-        x_ref, mix_ref, add_ref, bend_ref, high_ref, low_ref = refs[:6]
-        out_ref, line, spec = refs[6:]
+def owner_kernel(comps, keep, past, *refs):
+    x_ref, mix_ref, add_ref = refs[:3]
+    refs = refs[3:]
+    if past:
+        past_mix_ref, past_ref = refs[:2]
+        refs = refs[2:]
+    bend_ref, high_ref, low_ref, out_ref = refs[:4]
+    line, spec = refs[-2:]
     blocks = x_ref.shape[0]
     rows = blocks * SUBLANES
     width = 2 * LANES
     halves = (slice(0, LANES), slice(LANES, width))
-    for comp in range(3):
+    for comp in range(comps):
         own = slice(comp * LANES, (comp + 1) * LANES)
         reals, imags = butterfly(
             [x_ref[block, 0, :, own] for block in range(blocks)],
@@ -310,19 +311,21 @@
             line[comp].reshape(rows, width), high_ref[0], low_ref[0]
         ).reshape(blocks, SUBLANES, width)
     for part, half in enumerate(halves):
-        along, across, opening = (spec[comp, :, :, half] for comp in range(3))
-        line[0, :, :, half] = mix_ref[0] * along + mix_ref[1] * across + add_ref[0, part]
-        line[1, :, :, half] = mix_ref[1] * along + mix_ref[2] * across + add_ref[1, part]
-        line[2, :, :, half] = mix_ref[3] * opening + add_ref[2, part]
+        if comps == 1:
+            line[0, :, :, half] = mix_ref[0] * spec[0, :, :, half] + add_ref[0, part]
+            continue
+        along, across = spec[0, :, :, half], spec[1, :, :, half]
+        strike_sum = mix_ref[0] * along + mix_ref[1] * across + add_ref[0, part]
+        dip_sum = mix_ref[1] * along + mix_ref[2] * across + add_ref[1, part]
+        if past:
+            strike_sum += past_mix_ref[0] * past_ref[0, part] + past_mix_ref[1] * past_ref[1, part]
+            dip_sum += past_mix_ref[1] * past_ref[0, part] + past_mix_ref[2] * past_ref[1, part]
+        line[0, :, :, half] = strike_sum
+        line[1, :, :, half] = dip_sum
         if keep:
-            later_out_ref[0, part] = (
-                later_mix_ref[0] * along + later_mix_ref[1] * across + later_ref[0, part]
-            )
-            later_out_ref[1, part] = (
-                later_mix_ref[1] * along + later_mix_ref[2] * across + later_ref[1, part]
-            )
-            later_out_ref[2, part] = later_mix_ref[3] * opening + later_ref[2, part]
-    for comp in range(3):
+            refs[4][0, part] = along
+            refs[4][1, part] = across
+    for comp in range(comps):
         own = slice(comp * LANES, (comp + 1) * LANES)
         spec[comp] = split_product(
             line[comp].reshape(rows, width), high_ref[1], low_ref[1]
@@ -340,40 +343,35 @@
             out_ref[block, 1, :, own] = imags[block]
 
 
-def strike_pass(arrived, mixing, addend, tables, later=None):
+def strike_pass(arrived, mixing, addend, tables, past=(), keep=False):
     blocks, _, modes, depth = arrived.shape
-    bend, high, low = tables
-    tiles = modes // SUBLANES
+    comps = depth // LANES
     wide = pl.BlockSpec((blocks, 2, SUBLANES, depth), lambda tile: (0, 0, tile, 0))
-    factors = pl.BlockSpec((4, blocks, SUBLANES, LANES), lambda tile: (0, 0, tile, 0))
-    field = pl.BlockSpec((3, 2, blocks, SUBLANES, LANES), lambda tile: (0, 0, 0, tile, 0))
+    factors = pl.BlockSpec(
+        (mixing.shape[0], blocks, SUBLANES, LANES), lambda tile: (0, 0, tile, 0)
+    )
+    field = pl.BlockSpec((comps, 2, blocks, SUBLANES, LANES), lambda tile: (0, 0, 0, tile, 0))
     fixed = [
         pl.BlockSpec(item.shape, lambda tile, rank=item.ndim: (0,) * rank) for item in tables
     ]
-    operands = [arrived, mixing, addend]
-    in_specs = [wide, factors, field]
-    out_specs = [wide]
     out_shape = [jax.ShapeDtypeStruct(arrived.shape, jnp.float32)]
-    if later is not None:
-        operands += list(later)
-        in_specs += [factors, field]
-        out_specs.append(field)
+    if keep:
         out_shape.append(jax.ShapeDtypeStruct(addend.shape, jnp.float32))
     return pl.pallas_call(
-        functools.partial(owner_kernel, later is not None),
-        grid=(tiles,),
-        in_specs=in_specs + fixed,
-        out_specs=out_specs,
+        functools.partial(owner_kernel, comps, keep, bool(past)),
+        grid=(modes // SUBLANES,),
+        in_specs=[wide, factors, field] + [factors, field][: len(past)] + fixed,
+        out_specs=[wide, field][: len(out_shape)],
         out_shape=out_shape,
         scratch_shapes=[
-            pltpu.VMEM((3, blocks, SUBLANES, 2 * LANES), jnp.float32),
-            pltpu.VMEM((3, blocks, SUBLANES, 2 * LANES), jnp.float32),
+            pltpu.VMEM((comps, blocks, SUBLANES, 2 * LANES), jnp.float32),
+            pltpu.VMEM((comps, blocks, SUBLANES, 2 * LANES), jnp.float32),
         ],
         compiler_params=pltpu.CompilerParams(vmem_limit_bytes=40 * 1024 * 1024),
         cost_estimate=pl.CostEstimate(
             flops=12 * arrived.size * 2 * LANES, bytes_accessed=16 * arrived.size, transcendentals=0
         ),
-    )(*operands, bend, high, low)
+    )(arrived, mixing, addend, *past, *tables)
 
 
 def halves_of(table):
@@ -465,11 +463,11 @@
         moved = lax.all_to_all(
             dip_spec, ("strike", "dip"), split_axis=0, concat_axis=0, tiled=True
         )
-        return moved.reshape(devices, 2, modes, 3 * rows)
+        return moved.reshape(devices, 2, modes, -1)
 
     def receive(strike_rows):
         moved = lax.all_to_all(
-            strike_rows.reshape(2 * dip_cells, 3 * rows),
+            strike_rows.reshape(2 * dip_cells, -1),
             ("strike", "dip"),
             split_axis=0,
             concat_axis=0,
@@ -492,37 +490,93 @@
         wave_geometry(local_modes[None, :, None], residue + devices * step, dip_cells, strike_cells)
     )
     reach = jnp.transpose(by_residue(lengths), (2, 0, 1))
-    mixing = jnp.stack(sorted_mixing[0])
-    later_mixing = jnp.stack(sorted_mixing[1]) * (1 < reach).astype(jnp.float32)
+    reach = (1 < reach).astype(jnp.float32)
+    mixing = jnp.stack(sorted_mixing[0][:3])
+    past_mixing = jnp.stack(sorted_mixing[1][:3]) * reach
+    open_first, open_past = sorted_mixing[0][3], sorted_mixing[1][3] * reach
     plain_mixing = all_mixing(
         wave_geometry(local_modes[:, None], strike_modes[None, :], dip_cells, strike_cells)
     )
 
-    def past(first):
-        strike_sum, dip_sum, open_sum = 0.0, 0.0, 0.0
+    def sort(plain):
+        return jnp.transpose(by_residue(plain), (0, 3, 1, 2))
+
+    def lags(first):
         for offset in range(first, HIST):
-            along, cross, across, opening = plain_mixing[offset]
             active = (offset < lengths).astype(jnp.float32)
-            source = history[offset - first].astype(jnp.float32)
+            yield plain_mixing[offset], active, history[offset - first].astype(jnp.float32)
+
+    def past_shear(first):
+        strike_sum, dip_sum = 0.0, 0.0
+        for (along, cross, across, _), active, source in lags(first):
             strike_sum += (along * source[0] + cross * source[1]) * active
             dip_sum += (cross * source[0] + across * source[1]) * active
-            open_sum += opening * source[2] * active
-        summed = jnp.stack([strike_sum, dip_sum, open_sum])
-        return jnp.transpose(by_residue(summed), (0, 1, 4, 2, 3))
-
-    arrived = send(to_rows(slip_rate))
+        return jnp.stack([sort(strike_sum), sort(dip_sum)])
+
+    def past_open(first):
+        summed = 0.0
+        for (_, _, _, opening), active, source in lags(first):
+            summed += opening * source[2] * active
+        return sort(summed)
+
+    def mirror(spectrum):
+        flip = np.eye(rows, dtype=np.float32)[::-1]
+        apart = jnp.einsum(
+            "prim,mn->prin", spectrum[:, 1:][:, ::-1], flip, precision=lax.Precision.HIGHEST
+        )
+        whole = jnp.einsum(
+            "prim,mn->prin",
+            spectrum[:, :1],
+            np.roll(flip, 1, axis=1),
+            precision=lax.Precision.HIGHEST,
+        )
+        turned = jnp.concatenate([whole, apart], axis=1)
+        names = ("strike", "dip")
+        rest = lax.ppermute(
+            turned[:, :, 1:][:, :, ::-1], names, [(g, devices - 1 - g) for g in range(devices)]
+        )
+        edge = lax.ppermute(
+            turned[:, :, :1], names, [(g, (devices - g) % devices) for g in range(devices)]
+        )
+        both = jnp.concatenate([edge, rest], axis=2)
+        return jnp.stack([both[0], -both[1]])
+
+    slip_rows = to_rows(slip_rate)
+    shear = 2 * rows
+    arrived = send(slip_rows[:, :shear])
     load = jnp.concatenate(
         [prestress, (direct_effect * normal_stress)[None], state_log[None]]
     )
     load_strike, load_dip, strength, state = planes_of(to_rows(load))
-    strike_rows, addend = strike_pass(
-        arrived, mixing, past(1), tables, (later_mixing, past(2))
-    )
-    rates, state = friction_planes(receive(strike_rows), (load_strike, load_dip), strength, state)
-    (strike_rows,) = strike_pass(send(jnp.concatenate(rates, axis=1)), mixing, addend, tables)
-    rates, state = friction_planes(receive(strike_rows), (load_strike, load_dip), strength, state)
-    result = from_rows(jnp.concatenate(rates + [state], axis=1))
-    return (result[:3], result[3])
+    strike_rows, first_spec = strike_pass(arrived, mixing, past_shear(1), tables, keep=True)
+
+    open_earlier = past_open(1)
+    open_add = open_first * (open_earlier + mirror(open_earlier)) + past_open(2)
+    open_mix = 2.0 * open_first * open_first + open_past
+    (open_strike_rows,) = strike_pass(
+        send(slip_rows[:, shear:]), open_mix[None], open_add[None], tables
+    )
+    (open_force,) = receive(open_strike_rows)
+
+    load_rows = (load_strike, load_dip)
+    rates, state = friction_planes(receive(strike_rows), load_rows, strength, state)
+    arrived, open_force = lax.optimization_barrier(
+        (send(jnp.concatenate(rates, axis=1)), open_force)
+    )
+    open_rates = from_rows(open_force / radiation)
+    (strike_rows,) = strike_pass(
+        arrived,
+        mixing,
+        past_shear(2),
+        tables,
+        (past_mixing, first_spec),
+    )
+    rates, state = friction_planes(receive(strike_rows), load_rows, strength, state)
+    result, open_rates = lax.optimization_barrier(
+        (jnp.concatenate(rates + [state], axis=1), open_rates)
+    )
+    result = from_rows(result)
+    return (jnp.concatenate([result[:2], open_rates]), result[2])
 
 
 def choose(slip_rate, history, *others):

time: 452 us -> 472 us (1.044)
  blocking collectives: 178 us -> 23.1 us
  local copies, waits for them, and re-layouts: 69.6 us -> 127 us
  waiting for transfers between devices: 85 us -> 139 us
  starting transfers between devices: 21.2 us -> 69.7 us
  matrix products: 31.3 us -> 45.6 us
    all_to_all x2 -> x0, blocking collectives: 150 us -> none  [the longest x1 74.9 us: send(): lax.all_to_all(dip_spec, ('strike', 'dip'), split_axis=0, concat_axis=0,...]
    squeeze x0 -> x18, local copies, waits for them, and re-layouts: none -> 65.9 us  [the longest x12 43.3 us: past_shear(): strike_sum += (along * source[0] + cross * source[1]) * active]
    another operation x12 -> x0, local copies, waits for them, and re-layouts: 45.6 us -> none  [past(): summed = jnp.stack([strike_sum, dip_sum, open_sum])]
    all_to_all x1 -> x3, waiting for transfers between devices: 0.01 us -> 38.6 us  [send(): lax.all_to_all(dip_spec, ('strike', 'dip'), split_axis=0, concat_axis=0,...]
    all_to_all x1 -> x4, starting transfers between devices: 6.7 us -> 39.9 us  [the longest x3 36.4 us: receive(): lax.all_to_all(strike_rows.reshape(2 * dip_cells, -1), ('strike', 'dip'),...]
    ppermute x0 -> x2, waiting for transfers between devices: none -> 18.5 us  [the longest x1 18.5 us: mirror(): lax.ppermute(turned[:, :, 1:][:, :, ::-1], names, [(g, devices - 1 - g) f...]
    mul x0 -> x7, local copies, waits for them, and re-layouts: none -> 17 us  [past_shear(): strike_sum += (along * source[0] + cross * source[1]) * active]
    add x3 -> x0, other arithmetic: 14.4 us -> none  [the longest x1 6.68 us: past(): dip_sum += (cross * source[0] + across * source[1]) * active]
  transfers between devices with their start and end apart: 4 -> 11, of which waited for: 2 -> 8; matrix products, arithmetic and copies ran while one was open for 22% -> 42% of each run, Pallas kernels for 2% -> 2%
where the time goes in v3:
time: 472 us; the launch traced here: 466 us
  waiting for transfers between devices  139 us (29%)
  local copies, waits for them, and re-layouts  127 us (27%)
  starting transfers between devices  69.7 us (15%)
  other arithmetic  45.6 us (10%)
  matrix products  45.6 us (10%)
  blocking collectives  23.1 us (5%)
  Pallas kernels  13.9 us (3%)
    all_to_all x3, waiting for transfers between devices, receive(): lax.all_to_all(strike_rows.reshape(2 * dip_cells, -1), ('strike', 'dip'),...  57.5 us
    squeeze x12, local copies, waits for them, and re-layouts, past_shear(): strike_sum += (along * source[0] + cross * source[1]) * active  43.3 us
    all_to_all x3, waiting for transfers between devices, send(): lax.all_to_all(dip_spec, ('strike', 'dip'), split_axis=0, concat_axis=0,...  38.6 us
    all_to_all x3, starting transfers between devices, receive(): lax.all_to_all(strike_rows.reshape(2 * dip_cells, -1), ('strike', 'dip'),...  36.4 us
    all_to_all x2, waiting for transfers between devices, to_rows(): lax.all_to_all(parts, 'dip', split_axis=0, concat_axis=0, tiled=True)  24.3 us
    all_to_all x1, blocking collectives, from_rows(): lax.all_to_all(parts, 'dip', split_axis=0, concat_axis=0, tiled=True)  23.1 us
    squeeze x6, local copies, waits for them, and re-layouts, past_open(): summed += opening * source[2] * active  22.5 us
    dot_general x3, matrix products, receive(): return planes_of(jnp.dot(back_table, moved, precision=precise))  21.4 us
  transfers between devices with their start and end apart: 11, of which 8 were waited for; matrix products, arithmetic and copies ran while one was open for 42% of the time, Pallas kernels for 2%

profile of v3, /device:TPU:0, one launch (start us, length us, event | category | flops | bytes accessed | tf_op | source)
XLA Modules:
  0.0 465.6 jit_solution(3745594997234474862)
XLA Ops:
  3.3 4.3 all-to-all-start.1
  11.3 16.4 %all-to-all-done.1 = f32[4,256,384]{1,2,0:T(8,128)S(1)} async-done(((f32[4,256,384]{1,2,0:T(8,128)}), f32[4,256,384]{1,2,0:T(8,128)S(1)}, u32[]{:S(2)}, u32[]{:S(2)}) %all-to-all-start.1) | async-done | bytes 1572896 | tf_op jit(solution)/shard_map/all_to_all | solution.py:451
  28.9 3.6 all-to-all-start
  32.5 6.3 %slice_convert_fusion.2 = (f32[1,3,2,32,4096]{4,3,2,1,0:T(8,128)}, f32[1,3,2,32,4096]{4,3,2,1,0:T(8,128)}, f32[1,3,2,32,4096]{4,3,2,1,0:T(8,128)}) fusion(bf16[4,3,2,32,4096]{4,3,2,1,0:T(8,128)(2,1)} %param.15), kind=kLoop, calls=%fused_computation.10 | loop fusion | flops 2359296 | bytes 14155776 | tf_op jit(solution)/shard_map/convert_element_type | solution.py:507
  41.8 8.5 %fusion = f32[2048,256]{1,0:T(8,128)} fusion(f32[2048,1024]{1,0:T(8,128)} %constant.121.clone, f32[1024,384]{1,0:T(8,128)} %bitcast.133), kind=kOutput, calls=%fused_computation.13 | convolution fusion | flops 3221225472 | bytes 11534336 | tf_op jit(solution)/shard_map/dot_general | solution.py:462
  50.2 7.9 %all-to-all-done = f32[4,256,512]{1,2,0:T(8,128)S(1)} async-done(((f32[4,256,512]{1,2,0:T(8,128)}), f32[4,256,512]{1,2,0:T(8,128)S(1)}, u32[]{:S(2)}, u32[]{:S(2)}) %all-to-all-start) | async-done | bytes 2097184 | tf_op jit(solution)/shard_map/all_to_all | solution.py:451
  59.4 5.9 %all-to-all-start.2 = ((f32[32,64,256]{2,1,0:T(8,128)}), f32[32,64,256]{2,1,0:T(8,128)S(1)}, u32[]{:S(2)}, u32[]{:S(2)}) async-start(f32[32,64,256]{2,1,0:T(8,128)} %bitcast.126), calls=%async_computation.2 | async-start | bytes 4194304 | tf_op jit(solution)/shard_map/all_to_all | solution.py:463
  65.4 5.3 %fusion.78 = (f32[1,1,2,32,4096]{4,3,2,1,0:T(8,128)}, f32[1,1,2,32,4096]{4,3,2,1,0:T(8,128)}, f32[1,1,2,32,4096]{4,3,2,1,0:T(8,128)}, f32[1,1,2,32,4096]{4,3,2,1...) fusion(f32[1,3,2,32,4096]{4,3,2,1,0:T(8,128)} %get-tuple-element.22, ...), kind=kLoop, calls=%fused_computation.189 | loop fusion | bytes 12582912 | tf_op jit(solution)/shard_map/slice | solution.py:519
  70.6 3.8 squeeze.23
  74.4 3.7 copy.100
  78.1 3.8 squeeze.20
  81.9 3.7 copy.96
  85.6 3.8 squeeze.21
  89.3 3.7 copy.97
  95.8 3.7 copy.99
  99.5 3.5 fusion.80
  103.0 3.8 squeeze.24
  106.8 3.7 copy.102
  113.2 4.2 copy.103
  135.3 7.8 %fusion.64 = f32[2048,128]{1,0:T(8,128)} fusion(f32[2048,1024]{1,0:T(8,128)} %constant.121.clone, f32[1024,384]{1,0:T(8,128)} %bitcast.134), kind=kOutput, calls=%fused_computation.161 | convolution fusion | flops 1610612736 | bytes 9961472 | tf_op jit(solution)/shard_map/dot_general | solution.py:462
  143.1 6.0 %all-to-all-start.5 = ((f32[32,64,128]{2,1,0:T(8,128)}), f32[32,64,128]{2,1,0:T(8,128)S(1)}, u32[]{:S(2)}, u32[]{:S(2)}) async-start(f32[32,64,128]{2,1,0:T(8,128)} %bitcast.135), calls=%async_computation.5 | async-start | bytes 2097152 | tf_op jit(solution)/shard_map/all_to_all | solution.py:463
  149.1 5.5 %multiply_add_fusion.3 = (f32[1,32,32,128]{3,2,1,0:T(8,128)}, f32[1,32,32,128]{3,2,1,0:T(8,128)S(1)}, f32[1,32,32,128]{3,2,1,0:T(8,128)}, f32[1,32,32,128]{3,2,1...) fusion(f32[32]{0:T(128)S(1)} %get-tuple-element.73, f32[32,128]{1,0:T(8,128)S(1)} %get-tuple-element.71, ...), kind=kLoop, calls=%fused_computation.119 | loop fusion | flops 5505024 | bytes 3182880 | tf_op jit(solution)/shard_map/add | solution.py:421
  154.8 7.6 %fusion.24 = (f32[32,128,32]{1,0,2:T(8,128)}, f32[32,128,32]{1,0,2:T(8,128)}, f32[32,128,32]{1,0,2:T(8,128)S(1)}, f32[32,128,32]{1,0,2:T(8,128)S(1)}, f32[32,128...) fusion(f32[32]{0:T(128)S(1)} %get-tuple-element.73, ...), kind=kLoop, calls=%fused_computation.69 | loop fusion | flops 9568256 | bytes 6328608 | tf_op jit(solution)/shard_map/mul | solution.py:418
  166.8 4.9 %shard_map.149 = (f32[32,2,32,256]{3,2,1,0:T(8,128)S(1)}, f32[2,2,32,32,128]{4,3,2,1,0:T(8,128)S(1)}) custom-call(f32[32,2,32,256]{3,2,1,0:T(8,128)S(1)} %bitcast.113, f32[3,32,32,128]{3,2,1,0:T(8,128)S(1)} %pad_maximum_fusion.3.refs_1_, f32[2,2,32,32,128]{4,3,2,1,0:T(8,128)S(1)} %pad_maximum_fusion.1.refs_2_, f32[2,32,128]{2,1,0:T(8,128)S(1)} %copy-done.11, ...), custom_call_target="tpu_custom_call" | custom-call | flops 1610612736 | bytes 8388608 | tf_op jit(solution)/shard_map/pallas_call | solution.py:360
  175.3 5.2 %all-to-all-start.3 = ((f32[32,64,256]{2,1,0:T(8,128)}), f32[32,64,256]{2,1,0:T(8,128)}, u32[]{:S(2)}, u32[]{:S(2)}) async-start(f32[32,64,256]{2,1,0:T(8,128)} %bitcast.117), calls=%async_computation.3 | async-start | bytes 4194304 | tf_op jit(solution)/shard_map/all_to_all | solution.py:469
  180.6 3.8 squeeze.26
  184.4 3.7 copy.112
  188.1 3.8 squeeze.27
  191.9 3.7 copy.113
  195.6 3.8 squeeze.28
  199.4 3.7 copy.114
  203.1 3.5 add_bitcast_fusion.2
  221.2 5.3 %collective-permute-start.1 = (f32[2,32,31,128]{3,1,2,0:T(8,128)}, f32[2,32,31,128]{3,1,2,0:T(8,128)}, u32[]{:S(2)}, u32[]{:S(2)}) collective-permute-start(f32[2,32,31,128]{3,1,2,0:T(8,128)} %copy.115), channel_id=1, source_target_pairs={{0,31},{1,30},{2,29},{3,28},{4,27},{5,26},{6,25},{7,24},{8,23},{9,... | collective-permute-start | bytes 3047432 | tf_op jit(solution)/shard_map/ppermute | solution.py:535
  231.3 18.5 %collective-permute-done.1 = f32[2,32,31,128]{3,1,2,0:T(8,128)} collective-permute-done((f32[2,32,31,128]{3,1,2,0:T(8,128)}, f32[2,32,31,128]{3,1,2,0:T(8,128)}, u32[]{:S(2)}, u32[]{:S(2)}) %collective-permute-start.1) | collective-permute-done | bytes 1015840 | tf_op jit(solution)/shard_map/ppermute | solution.py:535
  252.6 3.4 shard_map.150
  257.0 27.2 %all-to-all-start.6 = ((f32[32,64,128]{2,1,0:T(8,128)}), f32[32,64,128]{2,1,0:T(8,128)}, u32[]{:S(2)}, u32[]{:S(2)}) async-start(f32[32,64,128]{2,1,0:T(8,128)} %bitcast.116), calls=%async_computation.6 | async-start | bytes 2097152 | tf_op jit(solution)/shard_map/all_to_all | solution.py:469
  286.2 7.4 %fusion.81 = f32[1024,256]{0,1:T(8,128)S(1)} fusion(f32[1024,2048]{1,0:T(8,128)} %constant.122.clone, f32[2048,256]{1,0:T(8,128)} %bitcast.18), kind=kOutput, calls=%fused_computation.192 | convolution fusion | flops 3221225472 | bytes 11534336 | tf_op jit(solution)/shard_map/dot_general | solution.py:476
  295.8 4.9 %fusion.2 = f32[2048,256]{1,0:T(8,128)} fusion(f32[2048,1024]{1,0:T(8,128)S(1)} %bitcast.119, f32[1024,128]{0,1:T(8,128)S(1)} %fusion.66, f32[1024,128]{0,1:T(8,128)S(1)} %get-tuple-element.16), kind=kOutput, calls=%fused_computation.15 | convolution fusion | flops 3221487616 | bytes 11534336 | tf_op jit(solution)/shard_map/dot_general | solution.py:462
  300.7 9.7 %all-to-all-done.6 = f32[32,64,128]{2,1,0:T(8,128)} async-done(((f32[32,64,128]{2,1,0:T(8,128)}), f32[32,64,128]{2,1,0:T(8,128)}, u32[]{:S(2)}, u32[]{:S(2)}) %all-to-all-start.6) | async-done | bytes 1048608 | tf_op jit(solution)/shard_map/all_to_all | solution.py:469
  310.4 4.0 all-to-all-start.4
  317.7 7.8 %fusion.83 = f32[1024,128]{1,0:T(8,128)} fusion(f32[1024,2048]{1,0:T(8,128)} %constant.122.clone, f32[2048,128]{1,0:T(8,128)} %bitcast.34), kind=kOutput, calls=%fused_computation.194 | convolution fusion | flops 1610612736 | bytes 9961472 | tf_op jit(solution)/shard_map/dot_general | solution.py:476
  325.5 37.7 %all-to-all-done.4 = f32[32,64,256]{2,1,0:T(8,128)} async-done(((f32[32,64,256]{2,1,0:T(8,128)}), f32[32,64,256]{2,1,0:T(8,128)}, u32[]{:S(2)}, u32[]{:S(2)}) %all-to-all-start.4) | async-done | bytes 2097184 | tf_op jit(solution)/shard_map/all_to_all | solution.py:463
  367.4 5.7 %shard_map.151 = f32[32,2,32,256]{3,2,1,0:T(8,128)S(1)} custom-call(f32[32,2,32,256]{3,2,1,0:T(8,128)} %bitcast.20.refs_0_, f32[3,32,32,128]{3,2,1,0:T(8,128)S(1)} %pad_maximum_fusion.3.refs_1_, f32[2,2,32,32,128]{4,3,2,1,0:T(8,128)S(1)} %copy-done.2, f32[3,32,32,128]{3,2,1,0:T(8,128)S(1)} %maximum_multiply_fusion.refs_3_, ...), custom_call_target="tpu_custom_call" | custom-call | flops 1610612736 | bytes 8388608 | tf_op jit(solution)/shard_map/pallas_call | solution.py:360
  374.4 4.0 all-to-all-start.7
  379.6 47.8 %all-to-all-done.7 = f32[32,64,256]{2,1,0:T(8,128)S(1)} async-done(((f32[32,64,256]{2,1,0:T(8,128)}), f32[32,64,256]{2,1,0:T(8,128)S(1)}, u32[]{:S(2)}, u32[]{:S(2)}) %all-to-all-start.7) | async-done | bytes 2097184 | tf_op jit(solution)/shard_map/all_to_all | solution.py:469
  427.3 3.5 all-to-all-start.8
  430.8 6.1 %fusion.84 = f32[1024,256]{0,1:T(8,128)S(1)} fusion(f32[1024,2048]{1,0:T(8,128)} %constant.122.clone, f32[2048,256]{1,0:T(8,128)S(1)} %bitcast.128), kind=kOutput, calls=%fused_computation.195 | convolution fusion | flops 3221225472 | bytes 11534336 | tf_op jit(solution)/shard_map/dot_general | solution.py:476
  439.8 23.1 %all_to_all.83 = f32[4,256,384]{1,2,0:T(8,128)S(1)} all-to-all(f32[4,256,384]{1,2,0:T(8,128)S(1)} %bitcast.132), channel_id=1, replica_groups=mesh['strike'=8,'dip'=4] {'dip'}, dimensions={0} | all-to-all | bytes 3145728 | tf_op jit(solution)/shard_map/all_to_all | solution.py:457
  (165 shorter events, 85.1 us)
Async XLA Ops:
  3.3 4.3 copy-start.46
  3.3 5.5 %copy-start.45 = (f32[2,512,256]{2,1,0:T(8,128)S(1)}, f32[2,512,256]{2,1,0:T(8,128)}, u32[]{:S(2)}) copy-start(f32[2,512,256]{2,1,0:T(8,128)} %param.17) | copy-start | bytes 3145732
  3.3 24.4 %all-to-all-start.1 = ((f32[4,256,384]{1,2,0:T(8,128)}), f32[4,256,384]{1,2,0:T(8,128)S(1)}, u32[]{:S(2)}, u32[]{:S(2)}) async-start(f32[4,256,384]{1,2,0:T(8,128)} %bitcast.9), calls=%async_computation.1 | async-start | bytes 3145728 | tf_op jit(solution)/shard_map/all_to_all | solution.py:451
  28.9 29.3 %all-to-all-start = ((f32[4,256,512]{1,2,0:T(8,128)}), f32[4,256,512]{1,2,0:T(8,128)S(1)}, u32[]{:S(2)}, u32[]{:S(2)}) async-start(f32[4,256,512]{1,2,0:T(8,128)} %bitcast.125), calls=%async_computation | async-start | bytes 4194304 | tf_op jit(solution)/shard_map/all_to_all | solution.py:451
  59.4 83.7 %all-to-all-start.2 = ((f32[32,64,256]{2,1,0:T(8,128)}), f32[32,64,256]{2,1,0:T(8,128)S(1)}, u32[]{:S(2)}, u32[]{:S(2)}) async-start(f32[32,64,256]{2,1,0:T(8,128)} %bitcast.126), calls=%async_computation.2 | async-start | bytes 4194304 | tf_op jit(solution)/shard_map/all_to_all | solution.py:463
  113.2 4.2 copy-start.47
  119.2 4.7 %copy-start.29 = (pred[32,128,32]{2,1,0:T(8,128)(4,1)}, pred[32,128,32]{2,1,0:T(8,128)(4,1)S(1)}, u32[]{:S(2)}) copy-start(pred[32,128,32]{2,1,0:T(8,128)(4,1)S(1)} %mul.2013) | copy-start | bytes 393220
  143.1 11.4 %copy-start = (f32[32,64,256]{2,1,0:T(8,128)}, f32[32,64,256]{2,1,0:T(8,128)S(1)}, u32[]{:S(2)}) copy-start(f32[32,64,256]{2,1,0:T(8,128)S(1)} %all-to-all-done.2) | copy-start | bytes 6291460
  143.1 32.2 %all-to-all-start.5 = ((f32[32,64,128]{2,1,0:T(8,128)}), f32[32,64,128]{2,1,0:T(8,128)S(1)}, u32[]{:S(2)}, u32[]{:S(2)}) async-start(f32[32,64,128]{2,1,0:T(8,128)} %bitcast.135), calls=%async_computation.5 | async-start | bytes 2097152 | tf_op jit(solution)/shard_map/all_to_all | solution.py:463
  154.6 7.8 %copy-start.36 = (f32[2,32,128,32]{2,1,3,0:T(8,128)S(1)}, f32[2,32,128,32]{2,1,3,0:T(8,128)}, u32[]{:S(2)}) copy-start(f32[2,32,128,32]{2,1,3,0:T(8,128)} %copy.102) | copy-start | bytes 3145732
  154.6 7.8 %copy-start.37 = (f32[2,32,128,32]{2,1,3,0:T(8,128)S(1)}, f32[2,32,128,32]{2,1,3,0:T(8,128)}, u32[]{:S(2)}) copy-start(f32[2,32,128,32]{2,1,3,0:T(8,128)} %copy.103) | copy-start | bytes 3145732
  154.7 7.7 %copy-start.21 = (f32[32,128,32]{1,0,2:T(8,128)S(1)}, f32[32,128,32]{1,0,2:T(8,128)}, u32[]{:S(2)}) copy-start(f32[32,128,32]{1,0,2:T(8,128)} %copy.101) | copy-start | bytes 1572868
  154.7 7.7 %copy-start.23 = (f32[32,128,32]{1,0,2:T(8,128)S(1)}, f32[32,128,32]{1,0,2:T(8,128)}, u32[]{:S(2)}) copy-start(f32[32,128,32]{1,0,2:T(8,128)} %copy.104) | copy-start | bytes 1572868
  154.7 7.7 %copy-start.28 = (f32[32,128,32]{1,0,2:T(8,128)S(1)}, f32[32,128,32]{1,0,2:T(8,128)}, u32[]{:S(2)}) copy-start(f32[32,128,32]{1,0,2:T(8,128)} %copy.98) | copy-start | bytes 1572868
  154.7 7.7 %copy-start.32 = (f32[2,32,128,32]{2,1,3,0:T(8,128)S(1)}, f32[2,32,128,32]{2,1,3,0:T(8,128)}, u32[]{:S(2)}) copy-start(f32[2,32,128,32]{2,1,3,0:T(8,128)} %copy.100) | copy-start | bytes 3145732
  154.7 7.7 %copy-start.33 = (f32[2,32,128,32]{2,1,3,0:T(8,128)S(1)}, f32[2,32,128,32]{2,1,3,0:T(8,128)}, u32[]{:S(2)}) copy-start(f32[2,32,128,32]{2,1,3,0:T(8,128)} %copy.96) | copy-start | bytes 3145732
  154.7 7.7 %copy-start.34 = (f32[2,32,128,32]{2,1,3,0:T(8,128)S(1)}, f32[2,32,128,32]{2,1,3,0:T(8,128)}, u32[]{:S(2)}) copy-start(f32[2,32,128,32]{2,1,3,0:T(8,128)} %copy.97) | copy-start | bytes 3145732
  154.8 7.7 %copy-start.35 = (f32[2,32,128,32]{2,1,3,0:T(8,128)S(1)}, f32[2,32,128,32]{2,1,3,0:T(8,128)}, u32[]{:S(2)}) copy-start(f32[2,32,128,32]{2,1,3,0:T(8,128)} %copy.99) | copy-start | bytes 3145732
  175.3 81.6 %all-to-all-start.3 = ((f32[32,64,256]{2,1,0:T(8,128)}), f32[32,64,256]{2,1,0:T(8,128)}, u32[]{:S(2)}, u32[]{:S(2)}) async-start(f32[32,64,256]{2,1,0:T(8,128)} %bitcast.117), calls=%async_computation.3 | async-start | bytes 4194304 | tf_op jit(solution)/shard_map/all_to_all | solution.py:469
  207.6 3.3 copy-start.49
  207.7 4.2 copy-start.48
  218.3 8.2 %copy-start.19 = (f32[2,31,32,128]{3,2,1,0:T(8,128)S(1)}, f32[2,31,32,128]{3,2,1,0:T(8,128)}, u32[]{:S(2)}) copy-start(f32[2,31,32,128]{3,2,1,0:T(8,128)} %copy-done.18) | copy-start | bytes 3047428
  221.2 28.5 %collective-permute-start.1 = (f32[2,32,31,128]{3,1,2,0:T(8,128)}, f32[2,32,31,128]{3,1,2,0:T(8,128)}, u32[]{:S(2)}, u32[]{:S(2)}) collective-permute-start(f32[2,32,31,128]{3,1,2,0:T(8,128)} %copy.115), channel_id=1, source_target_pairs={{0,31},{1,30},{2,29},{3,28},{4,27},{5,26},{6,25},{7,24},{8,23},{9,... | collective-permute-start | bytes 3047432 | tf_op jit(solution)/shard_map/ppermute | solution.py:535
  226.5 25.0 %collective-permute-start = (f32[2,32,1,128]{3,2,1,0:T(1,128)S(1)}, f32[2,32,1,128]{3,2,1,0:T(1,128)S(1)}, u32[]{:S(2)}, u32[]{:S(2)}) collective-permute-start(f32[2,32,1,128]{3,2,1,0:T(1,128)S(1)} %pad_maximum_fusion.8), channel_id=1, source_target_pairs={{0,0},{1,31},{2,30},{3,29},{4,28},{5,27},{6,26},{7,25},{8,24},{9,2... | collective-permute-start | bytes 98312 | tf_op jit(solution)/shard_map/ppermute | solution.py:538
  229.0 22.7 %copy-start.43 = (pred[32,128,32]{1,0,2:T(8,128)(4,1)}, pred[32,128,32]{1,0,2:T(8,128)(4,1)S(1)}, u32[]{:S(2)}) copy-start(pred[32,128,32]{1,0,2:T(8,128)(4,1)S(1)} %copy.111) | copy-start | bytes 393220
  229.0 22.7 %copy-start.30 = (f32[32,128,32]{1,0,2:T(8,128)S(1)}, f32[32,128,32]{1,0,2:T(8,128)}, u32[]{:S(2)}) copy-start(f32[32,128,32]{1,0,2:T(8,128)} %get-tuple-element.59) | copy-start | bytes 1572868
  229.0 22.7 %copy-start.31 = (f32[32,128,32]{1,0,2:T(8,128)S(1)}, f32[32,128,32]{1,0,2:T(8,128)}, u32[]{:S(2)}) copy-start(f32[32,128,32]{1,0,2:T(8,128)} %get-tuple-element.69) | copy-start | bytes 1572868
  231.2 20.5 %copy-start.14 = (f32[2,32,128,32]{2,1,3,0:T(8,128)S(1)}, f32[2,32,128,32]{2,1,3,0:T(8,128)}, u32[]{:S(2)}) copy-start(f32[2,32,128,32]{2,1,3,0:T(8,128)} %copy.112) | copy-start | bytes 3145732
  231.2 20.5 %copy-start.15 = (f32[2,32,128,32]{2,1,3,0:T(8,128)S(1)}, f32[2,32,128,32]{2,1,3,0:T(8,128)}, u32[]{:S(2)}) copy-start(f32[2,32,128,32]{2,1,3,0:T(8,128)} %copy.113) | copy-start | bytes 3145732
  231.2 20.5 %copy-start.17 = (f32[2,32,32,128]{3,2,1,0:T(8,128)S(1)}, f32[2,32,32,128]{3,2,1,0:T(8,128)}, u32[]{:S(2)}) copy-start(f32[2,32,32,128]{3,2,1,0:T(8,128)} %copy-done.16) | copy-start | bytes 3145732
  231.2 20.5 %copy-start.22 = (f32[32,128,32]{1,0,2:T(8,128)S(1)}, f32[32,128,32]{1,0,2:T(8,128)}, u32[]{:S(2)}) copy-start(f32[32,128,32]{1,0,2:T(8,128)} %copy.101) | copy-start | bytes 1572868
  231.3 20.5 %copy-start.24 = (f32[32,128,32]{1,0,2:T(8,128)S(1)}, f32[32,128,32]{1,0,2:T(8,128)}, u32[]{:S(2)}) copy-start(f32[32,128,32]{1,0,2:T(8,128)} %copy.104) | copy-start | bytes 1572868
  257.0 53.4 %all-to-all-start.6 = ((f32[32,64,128]{2,1,0:T(8,128)}), f32[32,64,128]{2,1,0:T(8,128)}, u32[]{:S(2)}, u32[]{:S(2)}) async-start(f32[32,64,128]{2,1,0:T(8,128)} %bitcast.116), calls=%async_computation.6 | async-start | bytes 2097152 | tf_op jit(solution)/shard_map/all_to_all | solution.py:469
  284.2 11.6 %slice-start = ((s8[8388608]{0:T(1024)(128)(4,1)}), s8[4194304]{0:T(1024)(128)(4,1)S(1)}, s32[]{:S(2)}) async-start(s8[8388608]{0:T(1024)(128)(4,1)} %bitcast.118), calls=%async_computation.10 | async-start | bytes 8388608
  286.2 9.3 %copy-start.12 = (f32[4,64,8,256]{3,2,0,1:T(8,128)}, f32[4,64,8,256]{3,2,0,1:T(8,128)S(1)}, u32[]{:S(2)}) copy-start(f32[4,64,8,256]{3,2,0,1:T(8,128)S(1)} %copy.134) | copy-start | bytes 6291460
  286.2 9.6 %slice-start.1 = ((s8[8388608]{0:T(1024)(128)(4,1)}), s8[4194304]{0:T(1024)(128)(4,1)S(1)}, s32[]{:S(2)}) async-start(s8[8388608]{0:T(1024)(128)(4,1)} %bitcast.118), calls=%async_computation.11 | async-start | bytes 8388608
  295.4 5.3 %copy-start.25 = (f32[1024,128]{0,1:T(8,128)}, f32[1024,128]{0,1:T(8,128)S(1)}, u32[]{:S(2)}) copy-start(f32[1024,128]{0,1:T(8,128)S(1)} %get-tuple-element.17) | copy-start | bytes 1572868
  310.4 4.0 copy-start.38
  310.4 52.9 %all-to-all-start.4 = ((f32[32,64,256]{2,1,0:T(8,128)}), f32[32,64,256]{2,1,0:T(8,128)}, u32[]{:S(2)}, u32[]{:S(2)}) async-start(f32[32,64,256]{2,1,0:T(8,128)} %bitcast.127), calls=%async_computation.4 | async-start | bytes 4194304 | tf_op jit(solution)/shard_map/all_to_all | solution.py:463
  314.4 3.0 copy-start.44
  314.4 3.0 copy-start.39
  314.4 3.0 copy-start.40
  314.4 3.0 copy-start.41
  374.4 4.0 copy-start.42
  374.4 52.9 %all-to-all-start.7 = ((f32[32,64,256]{2,1,0:T(8,128)}), f32[32,64,256]{2,1,0:T(8,128)S(1)}, u32[]{:S(2)}, u32[]{:S(2)}) async-start(f32[32,64,256]{2,1,0:T(8,128)} %bitcast.114), calls=%async_computation.7 | async-start | bytes 4194304 | tf_op jit(solution)/shard_map/all_to_all | solution.py:469
  427.3 12.3 %all-to-all-start.8 = ((f32[4,256,128]{1,2,0:T(8,128)}), f32[4,256,128]{1,2,0:T(8,128)S(1)}, u32[]{:S(2)}, u32[]{:S(2)}) async-start(f32[4,256,128]{1,2,0:T(8,128)} %bitcast.112), calls=%async_computation.8 | async-start | bytes 1048576 | tf_op jit(solution)/shard_map/all_to_all | solution.py:457
  430.8 6.2 %copy-start.13 = (f32[4,64,8,256]{3,2,0,1:T(8,128)S(1)}, f32[4,64,8,256]{3,2,0,1:T(8,128)}, u32[]{:S(2)}) copy-start(f32[4,64,8,256]{3,2,0,1:T(8,128)} %copy-done.12) | copy-start | bytes 6291460
  430.8 6.2 %copy-start.26 = (f32[1024,128]{0,1:T(8,128)S(1)}, f32[1024,128]{0,1:T(8,128)}, u32[]{:S(2)}) copy-start(f32[1024,128]{0,1:T(8,128)} %copy-done.25) | copy-start | bytes 1572868
  (15 other events, 20.1 us)

commit v4 on v3

--- a/solution.py
+++ b/solution.py
@@ -501,21 +501,21 @@
     def sort(plain):
         return jnp.transpose(by_residue(plain), (0, 3, 1, 2))
 
-    def lags(first):
+    def lags(first, older, reached):
         for offset in range(first, HIST):
-            active = (offset < lengths).astype(jnp.float32)
-            yield plain_mixing[offset], active, history[offset - first].astype(jnp.float32)
-
-    def past_shear(first):
+            active = (offset < reached).astype(jnp.float32)
+            yield plain_mixing[offset], active, older[offset - first].astype(jnp.float32)
+
+    def past_shear(first, older, reached):
         strike_sum, dip_sum = 0.0, 0.0
-        for (along, cross, across, _), active, source in lags(first):
+        for (along, cross, across, _), active, source in lags(first, older, reached):
             strike_sum += (along * source[0] + cross * source[1]) * active
             dip_sum += (cross * source[0] + across * source[1]) * active
         return jnp.stack([sort(strike_sum), sort(dip_sum)])
 
-    def past_open(first):
+    def past_open(first, older, reached):
         summed = 0.0
-        for (_, _, _, opening), active, source in lags(first):
+        for (_, _, _, opening), active, source in lags(first, older, reached):
             summed += opening * source[2] * active
         return sort(summed)
 
@@ -548,10 +548,11 @@
         [prestress, (direct_effect * normal_stress)[None], state_log[None]]
     )
     load_strike, load_dip, strength, state = planes_of(to_rows(load))
-    strike_rows, first_spec = strike_pass(arrived, mixing, past_shear(1), tables, keep=True)
-
-    open_earlier = past_open(1)
-    open_add = open_first * (open_earlier + mirror(open_earlier)) + past_open(2)
+    strike_rows, first_spec = strike_pass(arrived, mixing, past_shear(1, history, lengths), tables, keep=True)
+
+    strike_rows, older, reached = lax.optimization_barrier((strike_rows, history, lengths))
+    open_earlier = past_open(1, older, reached)
+    open_add = open_first * (open_earlier + mirror(open_earlier)) + past_open(2, older, reached)
     open_mix = 2.0 * open_first * open_first + open_past
     (open_strike_rows,) = strike_pass(
         send(slip_rows[:, shear:]), open_mix[None], open_add[None], tables
@@ -560,6 +561,7 @@
 
     load_rows = (load_strike, load_dip)
     rates, state = friction_planes(receive(strike_rows), load_rows, strength, state)
+    rates, older, reached = lax.optimization_barrier((rates, older, reached))
     arrived, open_force = lax.optimization_barrier(
         (send(jnp.concatenate(rates, axis=1)), open_force)
     )
@@ -567,7 +569,7 @@
     (strike_rows,) = strike_pass(
         arrived,
         mixing,
-        past_shear(2),
+        past_shear(2, older, reached),
         tables,
         (past_mixing, first_spec),
     )

time: 472 us -> 543 us (1.15)
  local copies, waits for them, and re-layouts: 127 us -> 174 us
  blocking collectives: 23.1 us -> 58.9 us
  other arithmetic: 45.6 us -> 67.6 us
  starting transfers between devices: 69.7 us -> 53.6 us
  waiting for transfers between devices: 139 us -> 124 us
    all_to_all x0 -> x1, blocking collectives: none -> 35.8 us  [receive(): lax.all_to_all(strike_rows.reshape(2 * dip_cells, -1), ('strike', 'dip'),...]
    squeeze x12 -> x20, local copies, waits for them, and re-layouts: 43.3 us -> 72.4 us  [past_shear(): strike_sum += (along * source[0] + cross * source[1]) * active]
    all_to_all x3 -> x2, waiting for transfers between devices: 57.5 us -> 85 us  [receive(): lax.all_to_all(strike_rows.reshape(2 * dip_cells, -1), ('strike', 'dip'),...]
    all_to_all x3 -> x2, starting transfers between devices: 36.4 us -> 9.7 us  [receive(): lax.all_to_all(strike_rows.reshape(2 * dip_cells, -1), ('strike', 'dip'),...]
    all_to_all x3, waiting for transfers between devices: 38.6 us -> 12.5 us  [send(): lax.all_to_all(dip_spec, ('strike', 'dip'), split_axis=0, concat_axis=0,...]
    mul x0 -> x6, local copies, waits for them, and re-layouts: none -> 18.3 us  [past_open(): summed += opening * source[2] * active]
    all_to_all x3, starting transfers between devices: 15.9 us -> 25.2 us  [send(): lax.all_to_all(dip_spec, ('strike', 'dip'), split_axis=0, concat_axis=0,...]
    another operation x3 -> x4, other arithmetic: 5.77 us -> 14.5 us  [past_shear(): return jnp.stack([sort(strike_sum), sort(dip_sum)])]
  transfers between devices with their start and end apart: 11 -> 10, of which waited for: 8 -> 5; matrix products, arithmetic and copies ran while one was open for 42% -> 45% of each run, Pallas kernels for 2% -> 2%
where the time goes in v4:
time: 543 us; the launch traced here: 537 us
  local copies, waits for them, and re-layouts  174 us (32%)
  waiting for transfers between devices  124 us (23%)
  other arithmetic  67.6 us (12%)
  blocking collectives  58.9 us (11%)
  starting transfers between devices  53.6 us (10%)
  matrix products  43.2 us (8%)
  Pallas kernels  14.5 us (3%)
    all_to_all x2, waiting for transfers between devices, receive(): lax.all_to_all(strike_rows.reshape(2 * dip_cells, -1), ('strike', 'dip'),...  85 us
    squeeze x20, local copies, waits for them, and re-layouts, past_shear(): strike_sum += (along * source[0] + cross * source[1]) * active  72.4 us
    all_to_all x1, blocking collectives, receive(): lax.all_to_all(strike_rows.reshape(2 * dip_cells, -1), ('strike', 'dip'),...  35.8 us
    all_to_all x3, starting transfers between devices, send(): lax.all_to_all(dip_spec, ('strike', 'dip'), split_axis=0, concat_axis=0,...  25.2 us
    all_to_all x1, blocking collectives, from_rows(): lax.all_to_all(parts, 'dip', split_axis=0, concat_axis=0, tiled=True)  23.1 us
    squeeze x6, local copies, waits for them, and re-layouts, past_open(): summed += opening * source[2] * active  22.6 us
    dot_general x3, matrix products, send(): dip_spec = jnp.dot(table, space_rows, precision=precise)  20.5 us
    mul x11, local copies, waits for them, and re-layouts, past_shear(): strike_sum += (along * source[0] + cross * source[1]) * active  19.9 us
  transfers between devices with their start and end apart: 10, of which 5 were waited for; matrix products, arithmetic and copies ran while one was open for 45% of the time, Pallas kernels for 2%

profile of v4, /device:TPU:0, one launch (start us, length us, event | category | flops | bytes accessed | tf_op | source)
XLA Modules:
  0.0 536.8 jit_solution(13260106133180331542)
XLA Ops:
  3.3 4.4 all-to-all-start.1
  7.7 5.0 slice_convert_fusion.4
  14.2 3.8 squeeze.76
  17.9 3.7 copy.118
  21.7 3.8 squeeze.75
  32.7 3.8 squeeze.74
  36.5 3.8 copy.115
  43.1 3.8 copy.114
  49.7 3.9 copy.112
  56.3 3.8 copy.111
  62.0 7.8 %fusion = f32[2048,256]{1,0:T(8,128)} fusion(f32[2048,1024]{1,0:T(8,128)} %constant.121.clone, f32[1024,384]{1,0:T(8,128)S(1)} %bitcast.138), kind=kOutput, calls=%fused_computation.15 | convolution fusion | flops 3221225472 | bytes 11534336 | tf_op jit(solution)/shard_map/dot_general | solution.py:462
  69.7 8.2 %all-to-all-start.2 = ((f32[32,64,256]{2,1,0:T(8,128)}), f32[32,64,256]{2,1,0:T(8,128)}, u32[]{:S(2)}, u32[]{:S(2)}) async-start(f32[32,64,256]{2,1,0:T(8,128)} %bitcast.11), calls=%async_computation.2 | async-start | bytes 4194304 | tf_op jit(solution)/shard_map/all_to_all | solution.py:463
  86.5 5.5 %multiply_add_fusion.3 = (f32[1,32,32,128]{3,2,1,0:T(8,128)}, f32[1,32,32,128]{3,2,1,0:T(8,128)S(1)}, f32[1,32,32,128]{3,2,1,0:T(8,128)}, f32[1,32,32,128]{3,2,1...) fusion(f32[32]{0:T(128)S(1)} %get-tuple-element.98, f32[32,128]{1,0:T(8,128)S(1)} %get-tuple-element.96, ...), kind=kLoop, calls=%fused_computation.121 | loop fusion | flops 5505024 | bytes 3182880 | tf_op jit(solution)/shard_map/add | solution.py:421
  92.1 7.8 %fusion.24 = (f32[32,128,32]{1,0,2:T(8,128)}, f32[32,128,32]{1,0,2:T(8,128)}, f32[32,128,32]{1,0,2:T(8,128)S(1)}, f32[32,128,32]{1,0,2:T(8,128)S(1)}, f32[32,128...) fusion(f32[32]{0:T(128)S(1)} %get-tuple-element.98, ...), kind=kLoop, calls=%fused_computation.71 | loop fusion | flops 9568256 | bytes 6328608 | tf_op jit(solution)/shard_map/mul | solution.py:418
  100.0 5.6 %add_bitcast_fusion.4 = (f32[1,2,32,32,128]{4,3,2,1,0:T(8,128)}, f32[1,2,32,32,128]{4,3,2,1,0:T(8,128)}) fusion(f32[2,32,128,32]{2,1,3,0:T(8,128)S(1)} %copy-done.33, f32[2,32,128,32]{2,1,3,0:T(8,128)S(1)} %copy-done.34, f32[2,32,128,32]{2,1,3,0:T(8,128)S(1)} %copy-done.35, f32[2,32,128,32]{2,1,3,0:T(8,128)S(1)} %copy-done.36, ...), kind=kLoop, calls=%fused_computation.31 | loop fusion | flops 7340032 | bytes 14680064 | tf_op jit(solution)/shard_map/stack | solution.py:514
  108.7 5.6 %fusion.64 = f32[2048,128]{1,0:T(8,128)} fusion(f32[2048,1024]{1,0:T(8,128)S(1)} %bitcast.126, f32[1024,384]{1,0:T(8,128)} %bitcast.139), kind=kOutput, calls=%fused_computation.171 | convolution fusion | flops 1610612736 | bytes 9961472 | tf_op jit(solution)/shard_map/dot_general | solution.py:462
  114.3 12.5 %all-to-all-done.2 = f32[32,64,256]{2,1,0:T(8,128)} async-done(((f32[32,64,256]{2,1,0:T(8,128)}), f32[32,64,256]{2,1,0:T(8,128)}, u32[]{:S(2)}, u32[]{:S(2)}) %all-to-all-start.2) | async-done | bytes 2097184 | tf_op jit(solution)/shard_map/all_to_all | solution.py:463
  126.8 12.7 %all-to-all-start.5 = ((f32[32,64,128]{2,1,0:T(8,128)}), f32[32,64,128]{2,1,0:T(8,128)S(1)}, u32[]{:S(2)}, u32[]{:S(2)}) async-start(f32[32,64,128]{2,1,0:T(8,128)} %bitcast.140), calls=%async_computation.5 | async-start | bytes 2097152 | tf_op jit(solution)/shard_map/all_to_all | solution.py:463
  141.1 5.5 %shard_map.149 = (f32[32,2,32,256]{3,2,1,0:T(8,128)S(1)}, f32[2,2,32,32,128]{4,3,2,1,0:T(8,128)S(1)}) custom-call(f32[32,2,32,256]{3,2,1,0:T(8,128)} %bitcast.12.refs_0_, f32[3,32,32,128]{3,2,1,0:T(8,128)S(1)} %pad_maximum_fusion.3.refs_1_, f32[2,2,32,32,128]{4,3,2,1,0:T(8,128)S(1)} %copy-done, f32[2,32,128]{2,1,0:T(8,128)S(1)} %copy-done.10, ...), custom_call_target="tpu_custom_call" | custom-call | flops 1610612736 | bytes 8388608 | tf_op jit(solution)/shard_map/pallas_call | solution.py:360
  146.7 4.3 slice_convert_fusion.7
  151.0 3.8 reshape.1475
  154.7 3.8 copy.131
  158.5 3.8 reshape.1473
  166.0 3.8 reshape.1471
  212.1 5.1 collective-permute-start.1
  219.7 4.9 all-to-all-start
  230.3 10.4 %collective-permute-done.1 = f32[2,32,31,128]{3,1,2,0:T(8,128)} collective-permute-done((f32[2,32,31,128]{3,1,2,0:T(8,128)}, f32[2,32,31,128]{3,1,2,0:T(8,128)}, u32[]{:S(2)}, u32[]{:S(2)}) %collective-permute-start.1) | collective-permute-done | bytes 1015840 | tf_op jit(solution)/shard_map/ppermute | solution.py:535
  247.9 16.0 %all-to-all-done = f32[4,256,512]{1,2,0:T(8,128)} async-done(((f32[4,256,512]{1,2,0:T(8,128)}), f32[4,256,512]{1,2,0:T(8,128)}, u32[]{:S(2)}, u32[]{:S(2)}) %all-to-all-start) | async-done | bytes 2097184 | tf_op jit(solution)/shard_map/all_to_all | solution.py:451
  263.9 35.8 %all_to_all.83 = f32[32,64,128]{2,1,0:T(8,128)} all-to-all(f32[32,64,128]{2,1,0:T(8,128)} %bitcast.123), channel_id=1, replica_groups=mesh['strike'=8,'dip'=4] {'strike','dip'}, dimensions={0} | all-to-all | bytes 2097152 | tf_op jit(solution)/shard_map/all_to_all | solution.py:469
  299.6 3.7 all-to-all-start.3
  308.4 6.6 %fusion.85 = f32[1024,128]{1,0:T(8,128)} fusion(f32[1024,2048]{1,0:T(8,128)} %constant.122.clone, f32[2048,128]{1,0:T(8,128)S(1)} %bitcast.141), kind=kOutput, calls=%fused_computation.206 | convolution fusion | flops 1610612736 | bytes 9961472 | tf_op jit(solution)/shard_map/dot_general | solution.py:476
  315.0 37.2 %all-to-all-done.3 = f32[32,64,256]{2,1,0:T(8,128)} async-done(((f32[32,64,256]{2,1,0:T(8,128)}), f32[32,64,256]{2,1,0:T(8,128)}, u32[]{:S(2)}, u32[]{:S(2)}) %all-to-all-start.3) | async-done | bytes 2097184 | tf_op jit(solution)/shard_map/all_to_all | solution.py:469
  352.3 6.8 %fusion.83 = f32[1024,256]{0,1:T(8,128)S(1)} fusion(f32[1024,2048]{1,0:T(8,128)} %constant.122.clone, f32[2048,256]{1,0:T(8,128)} %bitcast.18), kind=kOutput, calls=%fused_computation.204 | convolution fusion | flops 3221225472 | bytes 11534336 | tf_op jit(solution)/shard_map/dot_general | solution.py:476
  361.7 7.2 %fusion.2 = f32[2048,256]{1,0:T(8,128)} fusion(f32[2048,1024]{1,0:T(8,128)} %constant.121.clone, f32[1024,128]{0,1:T(8,128)S(1)} %get-tuple-element.20, f32[1024,128]{0,1:T(8,128)S(1)} %fusion.67), kind=kOutput, calls=%fused_computation.17 | convolution fusion | flops 3221487616 | bytes 11534336 | tf_op jit(solution)/shard_map/dot_general | solution.py:462
  368.9 4.3 all-to-all-start.4
  373.3 4.4 slice_convert_fusion.1
  379.2 3.8 squeeze.86
  383.0 3.7 copy.141
  386.7 3.8 squeeze.85
  397.3 3.8 squeeze.84
  401.0 3.7 copy.138
  404.8 3.8 squeeze.83
  426.7 4.4 add_bitcast_fusion.1
  436.8 5.7 %shard_map.151 = f32[32,2,32,256]{3,2,1,0:T(8,128)S(1)} custom-call(f32[32,2,32,256]{3,2,1,0:T(8,128)} %bitcast.20.refs_0_, f32[3,32,32,128]{3,2,1,0:T(8,128)S(1)} %pad_maximum_fusion.3.refs_1_, f32[2,2,32,32,128]{4,3,2,1,0:T(8,128)S(1)} %copy-done.2, f32[3,32,32,128]{3,2,1,0:T(8,128)S(1)} %maximum_multiply_fusion.refs_3_, ...), custom_call_target="tpu_custom_call" | custom-call | flops 1610612736 | bytes 8388608 | tf_op jit(solution)/shard_map/pallas_call | solution.py:360
  443.7 5.9 %all-to-all-start.7 = ((f32[32,64,256]{2,1,0:T(8,128)}), f32[32,64,256]{2,1,0:T(8,128)S(1)}, u32[]{:S(2)}, u32[]{:S(2)}) async-start(f32[32,64,256]{2,1,0:T(8,128)} %bitcast.121), calls=%async_computation.7 | async-start | bytes 4194304 | tf_op jit(solution)/shard_map/all_to_all | solution.py:469
  450.8 47.8 %all-to-all-done.7 = f32[32,64,256]{2,1,0:T(8,128)S(1)} async-done(((f32[32,64,256]{2,1,0:T(8,128)}), f32[32,64,256]{2,1,0:T(8,128)S(1)}, u32[]{:S(2)}, u32[]{:S(2)}) %all-to-all-start.7) | async-done | bytes 2097184 | tf_op jit(solution)/shard_map/all_to_all | solution.py:469
  502.3 6.1 %fusion.86 = f32[1024,256]{0,1:T(8,128)S(1)} fusion(f32[1024,2048]{1,0:T(8,128)} %constant.122.clone, f32[2048,256]{1,0:T(8,128)S(1)} %bitcast.133), kind=kOutput, calls=%fused_computation.207 | convolution fusion | flops 3221225472 | bytes 11534336 | tf_op jit(solution)/shard_map/dot_general | solution.py:476
  511.2 23.1 %all_to_all.84 = f32[4,256,384]{1,2,0:T(8,128)S(1)} all-to-all(f32[4,256,384]{1,2,0:T(8,128)S(1)} %bitcast.137), channel_id=1, replica_groups=mesh['strike'=8,'dip'=4] {'dip'}, dimensions={0} | all-to-all | bytes 3145728 | tf_op jit(solution)/shard_map/all_to_all | solution.py:457
  (187 shorter events, 146.8 us)
Async XLA Ops:
  3.3 56.8 %all-to-all-start.1 = ((f32[4,256,384]{1,2,0:T(8,128)}), f32[4,256,384]{1,2,0:T(8,128)}, u32[]{:S(2)}, u32[]{:S(2)}) async-start(f32[4,256,384]{1,2,0:T(8,128)} %bitcast.9), calls=%async_computation.1 | async-start | bytes 3145728 | tf_op jit(solution)/shard_map/all_to_all | solution.py:451
  36.5 3.8 copy-start.42
  49.7 3.9 copy-start.40
  62.0 7.8 %copy-start.20 = (f32[4,256,384]{2,1,0:T(8,128)}, f32[4,256,384]{2,1,0:T(8,128)S(1)}, u32[]{:S(2)}) copy-start(f32[4,256,384]{2,1,0:T(8,128)S(1)} %copy.110) | copy-start | bytes 4718596
  69.7 8.2 %copy-start.28 = (s32[32,4096]{1,0:T(8,128)S(1)}, s32[32,4096]{1,0:T(8,128)}, u32[]{:S(2)}) copy-start(s32[32,4096]{1,0:T(8,128)} %param.16) | copy-start | bytes 1572868
  69.7 57.0 %all-to-all-start.2 = ((f32[32,64,256]{2,1,0:T(8,128)}), f32[32,64,256]{2,1,0:T(8,128)}, u32[]{:S(2)}, u32[]{:S(2)}) async-start(f32[32,64,256]{2,1,0:T(8,128)} %bitcast.11), calls=%async_computation.2 | async-start | bytes 4194304 | tf_op jit(solution)/shard_map/all_to_all | solution.py:463
  86.5 13.5 %copy-start.38 = (f32[2,32,128,32]{2,1,3,0:T(8,128)S(1)}, f32[2,32,128,32]{2,1,3,0:T(8,128)}, u32[]{:S(2)}) copy-start(f32[2,32,128,32]{2,1,3,0:T(8,128)} %copy.111) | copy-start | bytes 3145732
  86.5 13.5 %copy-start.43 = (f32[32,128,32]{1,0,2:T(8,128)S(1)}, f32[32,128,32]{1,0,2:T(8,128)}, u32[]{:S(2)}) copy-start(f32[32,128,32]{1,0,2:T(8,128)} %copy.116) | copy-start | bytes 1572868
  91.9 8.0 %copy-start.35 = (f32[2,32,128,32]{2,1,3,0:T(8,128)S(1)}, f32[2,32,128,32]{2,1,3,0:T(8,128)}, u32[]{:S(2)}) copy-start(f32[2,32,128,32]{2,1,3,0:T(8,128)} %copy.115) | copy-start | bytes 3145732
  91.9 8.1 %copy-start.36 = (f32[2,32,128,32]{2,1,3,0:T(8,128)S(1)}, f32[2,32,128,32]{2,1,3,0:T(8,128)}, u32[]{:S(2)}) copy-start(f32[2,32,128,32]{2,1,3,0:T(8,128)} %copy.114) | copy-start | bytes 3145732
  91.9 8.1 %copy-start.37 = (f32[2,32,128,32]{2,1,3,0:T(8,128)S(1)}, f32[2,32,128,32]{2,1,3,0:T(8,128)}, u32[]{:S(2)}) copy-start(f32[2,32,128,32]{2,1,3,0:T(8,128)} %copy.112) | copy-start | bytes 3145732
  92.1 7.9 %copy-start.33 = (f32[2,32,128,32]{2,1,3,0:T(8,128)S(1)}, f32[2,32,128,32]{2,1,3,0:T(8,128)}, u32[]{:S(2)}) copy-start(f32[2,32,128,32]{2,1,3,0:T(8,128)} %copy.118) | copy-start | bytes 3145732
  92.1 7.9 %copy-start.34 = (f32[2,32,128,32]{2,1,3,0:T(8,128)S(1)}, f32[2,32,128,32]{2,1,3,0:T(8,128)}, u32[]{:S(2)}) copy-start(f32[2,32,128,32]{2,1,3,0:T(8,128)} %copy.117) | copy-start | bytes 3145732
  92.1 16.6 %slice-start = ((s8[8388608]{0:T(1024)(128)(4,1)}), s8[4194304]{0:T(1024)(128)(4,1)S(1)}, s32[]{:S(2)}) async-start(s8[8388608]{0:T(1024)(128)(4,1)} %bitcast.125), calls=%async_computation.10 | async-start | bytes 8388608
  99.9 5.7 %copy-start.21 = (f32[32,128,32]{1,0,2:T(8,128)}, f32[32,128,32]{1,0,2:T(8,128)S(1)}, u32[]{:S(2)}) copy-start(f32[32,128,32]{1,0,2:T(8,128)S(1)} %get-tuple-element.85) | copy-start | bytes 1572868
  99.9 5.7 %copy-start.22 = (f32[32,128,32]{1,0,2:T(8,128)}, f32[32,128,32]{1,0,2:T(8,128)S(1)}, u32[]{:S(2)}) copy-start(f32[32,128,32]{1,0,2:T(8,128)S(1)} %get-tuple-element.86) | copy-start | bytes 1572868
  99.9 5.7 %copy-start.23 = (f32[32,128,32]{1,0,2:T(8,128)}, f32[32,128,32]{1,0,2:T(8,128)S(1)}, u32[]{:S(2)}) copy-start(f32[32,128,32]{1,0,2:T(8,128)S(1)} %get-tuple-element.88) | copy-start | bytes 1572868
  99.9 5.7 %copy-start.24 = (f32[32,128,32]{1,0,2:T(8,128)}, f32[32,128,32]{1,0,2:T(8,128)S(1)}, u32[]{:S(2)}) copy-start(f32[32,128,32]{1,0,2:T(8,128)S(1)} %get-tuple-element.90) | copy-start | bytes 1572868
  99.9 5.7 %copy-start.25 = (f32[32,128,32]{1,0,2:T(8,128)}, f32[32,128,32]{1,0,2:T(8,128)S(1)}, u32[]{:S(2)}) copy-start(f32[32,128,32]{1,0,2:T(8,128)S(1)} %get-tuple-element.91) | copy-start | bytes 1572868
  99.9 5.7 %copy-start.26 = (f32[32,128,32]{1,0,2:T(8,128)}, f32[32,128,32]{1,0,2:T(8,128)S(1)}, u32[]{:S(2)}) copy-start(f32[32,128,32]{1,0,2:T(8,128)S(1)} %get-tuple-element.92) | copy-start | bytes 1572868
  100.0 8.7 %slice-start.1 = ((s8[8388608]{0:T(1024)(128)(4,1)}), s8[4194304]{0:T(1024)(128)(4,1)S(1)}, s32[]{:S(2)}) async-start(s8[8388608]{0:T(1024)(128)(4,1)} %bitcast.125), calls=%async_computation.11 | async-start | bytes 8388608
  114.3 25.2 %copy-start.4 = (bf16[2,256,256]{2,1,0:T(8,128)(2,1)S(1)}, bf16[2,256,256]{2,1,0:T(8,128)(2,1)}, u32[]{:S(2)}) copy-start(bf16[2,256,256]{2,1,0:T(8,128)(2,1)} %constant.124.clone.refs_4_.refs_6_) | copy-start | bytes 786436
  114.3 25.2 %copy-start.5 = (bf16[2,256,256]{2,1,0:T(8,128)(2,1)S(1)}, bf16[2,256,256]{2,1,0:T(8,128)(2,1)}, u32[]{:S(2)}) copy-start(bf16[2,256,256]{2,1,0:T(8,128)(2,1)} %constant.125.clone.refs_5_.refs_7_) | copy-start | bytes 786436
  114.3 25.2 %copy-start.10 = (f32[2,32,128]{2,1,0:T(8,128)S(1)}, f32[2,32,128]{2,1,0:T(8,128)}, u32[]{:S(2)}) copy-start(f32[2,32,128]{2,1,0:T(8,128)} %constant.123.clone.refs_3_.refs_5_) | copy-start | bytes 98308
  126.8 93.0 %all-to-all-start.5 = ((f32[32,64,128]{2,1,0:T(8,128)}), f32[32,64,128]{2,1,0:T(8,128)S(1)}, u32[]{:S(2)}, u32[]{:S(2)}) async-start(f32[32,64,128]{2,1,0:T(8,128)} %bitcast.140), calls=%async_computation.5 | async-start | bytes 2097152 | tf_op jit(solution)/shard_map/all_to_all | solution.py:463
  146.7 4.3 copy-start.7
  146.7 4.3 copy-start.8
  198.6 4.2 copy-start.47
  209.2 8.0 %copy-start.45 = (f32[512,256]{1,0:T(8,128)S(1)}, f32[512,256]{1,0:T(8,128)}, u32[]{:S(2)}) copy-start(f32[512,256]{1,0:T(8,128)} %mul.1978) | copy-start | bytes 1572868
  209.2 8.0 %copy-start.46 = (f32[2,512,256]{2,1,0:T(8,128)S(1)}, f32[2,512,256]{2,1,0:T(8,128)}, u32[]{:S(2)}) copy-start(f32[2,512,256]{2,1,0:T(8,128)} %param.17) | copy-start | bytes 3145732
  212.1 28.6 %collective-permute-start.1 = (f32[2,32,31,128]{3,1,2,0:T(8,128)}, f32[2,32,31,128]{3,1,2,0:T(8,128)}, u32[]{:S(2)}, u32[]{:S(2)}) collective-permute-start(f32[2,32,31,128]{3,1,2,0:T(8,128)} %copy.133), channel_id=1, source_target_pairs={{0,31},{1,30},{2,29},{3,28},{4,27},{5,26},{6,25},{7,24},{8,23},{9,... | collective-permute-start | bytes 3047432 | tf_op jit(solution)/shard_map/ppermute | solution.py:535
  219.7 44.1 %all-to-all-start = ((f32[4,256,512]{1,2,0:T(8,128)}), f32[4,256,512]{1,2,0:T(8,128)}, u32[]{:S(2)}, u32[]{:S(2)}) async-start(f32[4,256,512]{1,2,0:T(8,128)} %bitcast.131), calls=%async_computation | async-start | bytes 4194304 | tf_op jit(solution)/shard_map/all_to_all | solution.py:451
  227.4 15.1 %collective-permute-start = (f32[2,32,1,128]{3,2,1,0:T(1,128)S(1)}, f32[2,32,1,128]{3,2,1,0:T(1,128)S(1)}, u32[]{:S(2)}, u32[]{:S(2)}) collective-permute-start(f32[2,32,1,128]{3,2,1,0:T(1,128)S(1)} %pad_maximum_fusion.8), channel_id=1, source_target_pairs={{0,0},{1,31},{2,30},{3,29},{4,28},{5,27},{6,26},{7,25},{8,24},{9,2... | collective-permute-start | bytes 98312 | tf_op jit(solution)/shard_map/ppermute | solution.py:538
  228.0 14.6 %copy-start.31 = (f32[32,128,32]{1,0,2:T(8,128)S(1)}, f32[32,128,32]{1,0,2:T(8,128)}, u32[]{:S(2)}) copy-start(f32[32,128,32]{1,0,2:T(8,128)} %copy.132) | copy-start | bytes 1572868
  228.1 14.6 %copy-start.32 = (f32[32,128,32]{1,0,2:T(8,128)S(1)}, f32[32,128,32]{1,0,2:T(8,128)}, u32[]{:S(2)}) copy-start(f32[32,128,32]{1,0,2:T(8,128)} %copy.130) | copy-start | bytes 1572868
  230.2 12.4 %copy-start.13 = (f32[2,32,128,32]{2,1,3,0:T(8,128)S(1)}, f32[2,32,128,32]{2,1,3,0:T(8,128)}, u32[]{:S(2)}) copy-start(f32[2,32,128,32]{2,1,3,0:T(8,128)} %copy.129) | copy-start | bytes 3145732
  230.2 12.4 %copy-start.14 = (f32[2,32,128,32]{2,1,3,0:T(8,128)S(1)}, f32[2,32,128,32]{2,1,3,0:T(8,128)}, u32[]{:S(2)}) copy-start(f32[2,32,128,32]{2,1,3,0:T(8,128)} %copy.127) | copy-start | bytes 3145732
  230.3 12.4 %copy-start.16 = (f32[2,32,32,128]{3,2,1,0:T(8,128)S(1)}, f32[2,32,32,128]{3,2,1,0:T(8,128)}, u32[]{:S(2)}) copy-start(f32[2,32,32,128]{3,2,1,0:T(8,128)} %copy-done.15) | copy-start | bytes 3145732
  230.3 12.4 %copy-start.29 = (f32[32,128,32]{1,0,2:T(8,128)S(1)}, f32[32,128,32]{1,0,2:T(8,128)}, u32[]{:S(2)}) copy-start(f32[32,128,32]{1,0,2:T(8,128)} %get-tuple-element.84) | copy-start | bytes 1572868
  230.3 12.4 %copy-start.30 = (f32[32,128,32]{1,0,2:T(8,128)S(1)}, f32[32,128,32]{1,0,2:T(8,128)}, u32[]{:S(2)}) copy-start(f32[32,128,32]{1,0,2:T(8,128)} %get-tuple-element.94) | copy-start | bytes 1572868
  299.6 52.6 %all-to-all-start.3 = ((f32[32,64,256]{2,1,0:T(8,128)}), f32[32,64,256]{2,1,0:T(8,128)}, u32[]{:S(2)}, u32[]{:S(2)}) async-start(f32[32,64,256]{2,1,0:T(8,128)} %bitcast.124), calls=%async_computation.3 | async-start | bytes 4194304 | tf_op jit(solution)/shard_map/all_to_all | solution.py:469
  352.3 6.8 %copy-start.11 = (f32[4,64,8,256]{3,2,0,1:T(8,128)S(1)}, f32[4,64,8,256]{3,2,0,1:T(8,128)}, u32[]{:S(2)}) copy-start(f32[4,64,8,256]{3,2,0,1:T(8,128)} %copy.154) | copy-start | bytes 6291460
  368.9 63.7 %all-to-all-start.4 = ((f32[32,64,256]{2,1,0:T(8,128)}), f32[32,64,256]{2,1,0:T(8,128)}, u32[]{:S(2)}, u32[]{:S(2)}) async-start(f32[32,64,256]{2,1,0:T(8,128)} %bitcast.132), calls=%async_computation.4 | async-start | bytes 4194304 | tf_op jit(solution)/shard_map/all_to_all | solution.py:463
  443.7 6.0 %copy-start.44 = (f32[1024,128]{1,0:T(8,128)S(1)}, f32[1024,128]{1,0:T(8,128)}, u32[]{:S(2)}) copy-start(f32[1024,128]{1,0:T(8,128)} %fusion.85) | copy-start | bytes 1572868
  443.7 54.8 %all-to-all-start.7 = ((f32[32,64,256]{2,1,0:T(8,128)}), f32[32,64,256]{2,1,0:T(8,128)S(1)}, u32[]{:S(2)}, u32[]{:S(2)}) async-start(f32[32,64,256]{2,1,0:T(8,128)} %bitcast.121), calls=%async_computation.7 | async-start | bytes 4194304 | tf_op jit(solution)/shard_map/all_to_all | solution.py:469
  498.6 12.5 %all-to-all-start.8 = ((f32[4,256,128]{1,2,0:T(8,128)}), f32[4,256,128]{1,2,0:T(8,128)S(1)}, u32[]{:S(2)}, u32[]{:S(2)}) async-start(f32[4,256,128]{1,2,0:T(8,128)} %bitcast.120), calls=%async_computation.8 | async-start | bytes 1048576 | tf_op jit(solution)/shard_map/all_to_all | solution.py:457
  502.3 6.2 %copy-start.12 = (f32[4,64,8,256]{3,2,0,1:T(8,128)S(1)}, f32[4,64,8,256]{3,2,0,1:T(8,128)}, u32[]{:S(2)}) copy-start(f32[4,64,8,256]{3,2,0,1:T(8,128)} %copy.154) | copy-start | bytes 6291460
  502.3 6.2 %copy-start.19 = (f32[1024,128]{0,1:T(8,128)S(1)}, f32[1024,128]{0,1:T(8,128)}, u32[]{:S(2)}) copy-start(f32[1024,128]{0,1:T(8,128)} %copy-done.18) | copy-start | bytes 1572868
  (13 other events, 23.0 us)
